TPU v7x, 32 devices: a whole 2x2x4 slice. The times are simulated.
32 devices in a mesh: blk: 4 (over z), lat: 8 (over y, x, core).
Axes of the slice: x: 2, y: 2, z: 4, core: 2. Of those that a mesh axis runs over, the one named last changes fastest.
Arguments:
- ice_area: float32 [5, 12, 256, 4096], P(None, None, 'lat', 'blk'), may hold values from 0.05 to 1
- departure_weights: int32 [9, 256, 4096], P(None, 'lat', 'blk'), may hold values from 0 to 4096, as said below
- weld_rate: float32 [256, 4096], P('lat', 'blk'), may hold values from 0.1 to 1
- ice_cover: int32 [256, 4], P('lat', 'blk'), may hold values from 0 to 1, as said below
- wave_ocean: float32 [32, 25, 32, 1024], P(('blk', 'lat')), may hold values from 0.02 to 0.5
- ocean_route: int32 [32, 32], P(('blk', 'lat')), may hold values from 0 to 31, each once within a row
Outputs:
- new_area: float32 [5, 12, 256, 4096], P(None, None, 'lat', 'blk')
Inputs may be any that keep to these rules, and one draw needn't show every extreme that they name: `departure_weights`: the nine weights of a cell sum to 4096; each off-centre weight is below 410. `ice_cover`: each device's count of ice-covered rows is a multiple of 4, from 4 to 32; in every longitude band the 8 devices' counts are 4, 8, ..., 32 in some order, so a band holds exactly 144 ice-covered blocks. `ocean_route`: each row is a permutation: every ocean device sends one wave block to every ice device.
All inputs are finite; a program needn't handle non-finite values.
Results may differ from a plain program's by a relative error of at most 0.0001.
Values sent between devices are 32-bit elements; how exact they have to be, the bound alone decides.
No kernel may reach another device: no remote copies, remote signals or barrier semaphores. Data moves between devices by JAX's collectives and lax.ppermute only.
A program may use at most 192 MiB of HBM per device.

v0:
```python
import functools

import jax
import jax.numpy as jnp
import ml_dtypes
import numpy as np
from jax import lax
from jax.experimental import pallas as pl
from jax.experimental.pallas import tpu as pltpu
from jax.sharding import PartitionSpec as P

NCAT = 5
NFSD = 12
FREQ = 25
PLANES = NCAT * NFSD
LANES = 128
SUB = 8
PITCH = 24
EXT = 48
AXES = ("blk", "lat")

fracture_step = 0.1
weld_scale = 840.0 / 1024.0


def weld_table():
    index = np.arange(NFSD)
    apart = index[:, None] - index[None, :]
    exact = np.where(apart > 0, 1.0, -1.0) / (1.0 + np.abs(apart)) * weld_scale
    high = exact.astype(ml_dtypes.bfloat16).astype(np.float64)
    low = exact - high
    kept = [0, 1, 2, 3, 8, 9, 10, 11]
    assert not np.delete(low, kept, axis=1).any()
    joined = np.concatenate([high, high, low[:, kept]], axis=1)
    return np.kron(joined, np.eye(SUB)).astype(ml_dtypes.bfloat16)


def pack_kernel(
    blk_count, lat_count, wave, ice, route, message, rows_a, rows_b,
    wave_buf, west_buf, east_buf, sums, columns, wave_sem, col_sem, row_sem,
):
    freq_count, dests, cells = wave.shape
    parts = wave_sem.shape[0]
    step = freq_count // parts
    tile_cols = ice.shape[2]
    tile_rows = ice.shape[1]
    chunks = tile_cols // LANES
    me_b = lax.axis_index("blk")
    me_l = lax.axis_index("lat")

    col_copies = [
        pltpu.make_async_copy(ice.at[:, :, pl.ds(0, LANES)], west_buf, col_sem.at[0]),
        pltpu.make_async_copy(
            ice.at[:, :, pl.ds(tile_cols - LANES, LANES)], east_buf, col_sem.at[1]
        ),
    ]
    wave_copies = [
        pltpu.make_async_copy(
            wave.at[pl.ds(p * step, step)], wave_buf.at[pl.ds(p * step, step)], wave_sem.at[p]
        )
        for p in range(parts)
    ]
    odd = lax.rem(me_l, 2) == 1
    first = jnp.where(odd, 0, tile_rows - 1)
    second = jnp.where(odd, tile_rows - 1, 0)
    row_copies = []
    for j in range(chunks):
        for which, (row, out) in enumerate(((first, rows_a), (second, rows_b))):
            row_copies.append(
                pltpu.make_async_copy(
                    ice.at[:, row, pl.ds(j * LANES, LANES)],
                    out.at[j, pl.ds(0, PLANES), :],
                    row_sem.at[which, j],
                )
            )
    for copy in col_copies + wave_copies + row_copies:
        copy.start()

    lane = lax.broadcasted_iota(jnp.int32, (SUB, LANES), 1)
    for side, (buf, from_lane) in enumerate(((west_buf, 0), (east_buf, LANES - 1))):
        col_copies[side].wait()

        def gather(p, parts_of):
            shift = lax.rem(p - from_lane + LANES, LANES)
            return tuple(
                jnp.where(lane == p, pltpu.roll(buf[p, SUB * i : SUB * i + SUB, :], shift, 1), part)
                for i, part in enumerate(parts_of)
            )

        got = tuple(jnp.zeros((SUB, LANES), jnp.float32) for _ in range(tile_rows // SUB))
        got = lax.fori_loop(0, PLANES, gather, got, unroll=4)
        half = len(got) // 2
        for i in range(half):
            columns[side, SUB * i : SUB * i + SUB, :] = jnp.where(
                lane < 64, got[i], pltpu.roll(got[i + half], 64, 1)
            )

    def send_columns(d, _):
        to_b = d // lat_count
        last_col = (to_b == lax.rem(me_b + 1, blk_count)) | (
            to_b == lax.rem(2 * blk_count - 2 - me_b, blk_count)
        )
        side = jnp.where(last_col, 1, 0)
        for i in range(2):
            message[d, SUB + SUB * i : 2 * SUB + SUB * i, :] = columns[side, SUB * i : SUB * i + SUB, :]
        return 0

    lax.fori_loop(0, dests, send_columns, 0, unroll=4)

    for copy in wave_copies:
        copy.wait()
    pieces = cells // LANES
    for group in range(dests // SUB):
        for j in range(pieces):
            total = jnp.zeros((SUB, LANES), jnp.float32)
            for f in range(freq_count):
                total = total + wave_buf[
                    f, SUB * group : SUB * group + SUB, LANES * j : LANES * j + LANES
                ] * np.float32((f + 1.0) / freq_count)
            sums[pl.ds(SUB * SUB * group + j, SUB, stride=SUB), :] = total

    def send_sums(m, _):
        message[route[0, m], 0:SUB, :] = sums[pl.ds(pl.multiple_of(m * SUB, SUB), SUB), :]
        return 0

    lax.fori_loop(0, dests, send_sums, 0, unroll=4)
    for copy in row_copies:
        copy.wait()


def pack(ice, wave, route, blk_count, lat_count):
    planes, tile_rows, tile_cols = ice.shape
    freq_count, dests, cells = wave.shape
    chunks = tile_cols // LANES
    return pl.pallas_call(
        functools.partial(pack_kernel, blk_count, lat_count),
        out_shape=(
            jax.ShapeDtypeStruct((dests, PITCH, LANES), jnp.float32),
            jax.ShapeDtypeStruct((chunks, 64, LANES), jnp.float32),
            jax.ShapeDtypeStruct((chunks, 64, LANES), jnp.float32),
        ),
        in_specs=[
            pl.BlockSpec(memory_space=pl.ANY),
            pl.BlockSpec(memory_space=pl.ANY),
            pl.BlockSpec(memory_space=pltpu.SMEM),
        ],
        out_specs=(
            pl.BlockSpec(memory_space=pltpu.VMEM),
            pl.BlockSpec(memory_space=pl.ANY),
            pl.BlockSpec(memory_space=pl.ANY),
        ),
        scratch_shapes=[
            pltpu.VMEM((freq_count, dests, cells), jnp.float32),
            pltpu.VMEM((planes, tile_rows, LANES), jnp.float32),
            pltpu.VMEM((planes, tile_rows, LANES), jnp.float32),
            pltpu.VMEM((dests * SUB, LANES), jnp.float32),
            pltpu.VMEM((2, 16, LANES), jnp.float32),
            pltpu.SemaphoreType.DMA((5,)),
            pltpu.SemaphoreType.DMA((2,)),
            pltpu.SemaphoreType.DMA((2, chunks)),
        ],
        compiler_params=pltpu.CompilerParams(vmem_limit_bytes=24 * 1024 * 1024),
        name="pack",
    )(wave, ice, route)


def step_kernel(
    blk_count, lat_count, cells,
    cover, ice, weights, weld, received, rows_a, rows_b, table, out,
    ext, scaled, weld_now, rate, ghosts, cols, moved,
):
    n = pl.program_id(0)
    tile_rows, tile_cols = weld.shape
    bands = tile_rows // SUB
    chunks = tile_cols // LANES
    plane_pitch = chunks * EXT
    lane = lax.broadcasted_iota(jnp.int32, (SUB, LANES), 1)
    sublane = lax.broadcasted_iota(jnp.int32, (SUB, LANES), 0)
    me_b = lax.axis_index("blk")
    me_l = lax.axis_index("lat")

    def shifted(pieces, west, east):
        to_right = [pltpu.roll(piece, 1, 1) for piece in pieces]
        to_left = [pltpu.roll(piece, LANES - 1, 1) for piece in pieces]
        from_west = [
            jnp.where(lane == 0, to_right[j - 1] if j else west, to_right[j])
            for j in range(chunks)
        ]
        from_east = [
            jnp.where(lane == LANES - 1, to_left[j + 1] if j + 1 < chunks else east, to_left[j])
            for j in range(chunks)
        ]
        return from_west, pieces, from_east

    @pl.when(n == 0)
    def prepare():
        top = me_l == lat_count - 1
        bottom = me_l == 0
        odd = lax.rem(me_l, 2) == 1
        west_b = lax.rem(me_b + blk_count - 1, blk_count)
        east_b = lax.rem(me_b + 1, blk_count)
        above_l = jnp.minimum(me_l + 1, lat_count - 1)
        below_l = jnp.maximum(me_l - 1, 0)

        def block(b, l):
            return pl.multiple_of((b * lat_count + l) * PITCH + SUB, SUB)

        for side, b in enumerate((west_b, east_b)):
            start = block(b, me_l)
            for i in range(2):
                packed = received[pl.ds(start + SUB * i, SUB), :]
                cols[side, SUB * i : SUB * i + SUB, :] = packed
                cols[side, 16 + SUB * i : 16 + SUB * i + SUB, :] = pltpu.roll(packed, 64, 1)

        def corner(b, l, last_row):
            start = block(b, l)
            low = received[pl.ds(start, SUB), :][0:1, :]
            high = pltpu.roll(received[pl.ds(start + SUB, SUB), :], 64, 1)[7:8, :]
            line = jnp.where(last_row, high, low)
            spread = jnp.broadcast_to(line, (SUB, LANES))
            return [
                jnp.sum(jnp.where(lane == SUB * q + sublane, spread, 0.0), axis=1, keepdims=True)
                for q in range(SUB)
            ]

        below_corners = [corner(b, below_l, True) for b in (west_b, east_b)]
        above_corners = [
            corner(jnp.where(top, fold_b, b), above_l, top)
            for fold_b, b in (
                (lax.rem(blk_count - me_b, blk_count), west_b),
                (lax.rem(2 * blk_count - 2 - me_b, blk_count), east_b),
            )
        ]
        backwards = LANES - 1 - lane
        for q in range(SUB):
            band = pl.ds(SUB * q, SUB)
            below = [
                jnp.where(bottom, 0.0, jnp.where(odd, rows_a[j, band, :], rows_b[j, band, :]))
                for j in range(chunks)
            ]
            above = [
                jnp.where(odd, rows_b[j, band, :], rows_a[j, band, :]) for j in range(chunks)
            ]
            folded = [
                jnp.take_along_axis(above[chunks - 1 - j], backwards, axis=1)
                for j in range(chunks)
            ]
            above = [jnp.where(top, folded[j], above[j]) for j in range(chunks)]
            for side, (pieces, corners) in enumerate(
                ((below, below_corners), (above, above_corners))
            ):
                ends = [jnp.broadcast_to(corners[s][q], (SUB, LANES)) for s in range(2)]
                if side == 0:
                    ends = [jnp.where(bottom, 0.0, end) for end in ends]
                for dx, line in enumerate(shifted(pieces, *ends)):
                    for j in range(chunks):
                        ghosts[side, dx, j, band, :] = line[j]

        per_row = tile_cols // cells
        for i in range(bands):
            mask = jnp.zeros((SUB, LANES), jnp.float32)
            for r in range(SUB):
                here = (cover[0, SUB * i + r] > 0).astype(jnp.float32)
                mask = jnp.where(sublane == r, here, mask)
            for j in range(chunks):
                own = (slice(SUB * i, SUB * i + SUB), slice(LANES * j, LANES * j + LANES))
                first = (per_row * SUB * i + j * LANES // cells) * PITCH + j % (cells // LANES)
                got = received[pl.ds(first, SUB, stride=per_row * PITCH), :]
                rate[own] = got * mask
                weld_now[own] = weld[own] * mask * np.float32(0.06 / weld_scale)
                for w in range(9):
                    scaled[(w,) + own] = weights[(w,) + own].astype(jnp.float32) * np.float32(
                        1.0 / 4096.0
                    )

    plane0 = n * NFSD
    for side in range(2):
        row = 7 if side == 0 else 8 + tile_rows
        for dx in range(3):
            for j in range(chunks):
                for k0 in (0, NFSD - SUB):
                    ext[dx, pl.ds(k0 * plane_pitch + j * EXT + row, SUB, stride=plane_pitch), :] = (
                        ghosts[side, dx, j, pl.ds(plane0 + k0, SUB), :]
                    )

    def widen(k, _):
        p = plane0 + k
        for i in range(bands):
            pieces = [
                ice[k, SUB * i : SUB * i + SUB, LANES * j : LANES * j + LANES]
                for j in range(chunks)
            ]
            west = pltpu.roll(cols[0, SUB * i : SUB * i + SUB, :], LANES - p, 1)
            east = pltpu.roll(cols[1, SUB * i : SUB * i + SUB, :], LANES - 1 - p, 1)
            for dx, line in enumerate(shifted(pieces, west, east)):
                for j in range(chunks):
                    start = pl.multiple_of(k * plane_pitch + j * EXT + SUB + SUB * i, SUB)
                    ext[dx, pl.ds(start, SUB), :] = line[j]
        return 0

    lax.fori_loop(0, NFSD, widen, 0)

    share = np.float32(fracture_step / 11.0) / (1.0 + 0.5 * n.astype(jnp.float32))

    def cells_of(i, jj, width):
        span = LANES * width
        rows = pl.ds(pl.multiple_of(i * SUB, SUB), SUB)
        for s in range(width):
            j = jj * width + s
            columns = pl.ds(pl.multiple_of(j * LANES, LANES), LANES)
            factors = [scaled[w, rows, columns] for w in range(9)]
            for k in range(NFSD):
                total = None
                for w in range(9):
                    dy, dx = w // 3, w % 3
                    start = k * plane_pitch + j * EXT + i * SUB + 7 + dy
                    term = factors[w] * ext[dx, pl.ds(start, SUB), :]
                    total = term if total is None else total + term
                moved[SUB * k : SUB * k + SUB, LANES * s : LANES * s + LANES] = total
        whole = moved[...]
        high = whole.astype(jnp.bfloat16)
        low = (whole - high.astype(jnp.float32)).astype(jnp.bfloat16)
        stacked = jnp.concatenate([high, low, high[: 4 * SUB], high[8 * SUB :]], axis=0)
        exchange = jnp.dot(table[...], stacked, preferred_element_type=jnp.float32)
        columns = pl.ds(pl.multiple_of(jj * span, span), span)
        speed = weld_now[rows, columns]
        breaking = rate[rows, columns] * share
        carried = jnp.zeros((SUB, span), jnp.float32)
        welded = []
        own = [moved[SUB * k : SUB * k + SUB, :] for k in range(NFSD)]
        squares = [area * (area * np.float32(weld_scale)) for area in own]
        for k in range(NFSD):
            turn = own[k] * exchange[SUB * k : SUB * k + SUB, :]
            if k:
                turn = turn + squares[k - 1]
            if k == NFSD - 1:
                turn = turn + squares[k]
            welded.append(own[k] + speed * turn)
        for k in range(NFSD - 1, -1, -1):
            broken = breaking * welded[k]
            out[k, rows, columns] = welded[k] + (carried - np.float32(k) * broken)
            carried = carried + broken

    width = 2

    def tiles(t, _):
        cells_of(t // (chunks // width), lax.rem(t, chunks // width), width)
        return 0

    lax.fori_loop(0, bands * (chunks // width), tiles, 0)


def advance(cover, ice, weights, weld, received, rows_a, rows_b, blk_count, lat_count, cells):
    planes, tile_rows, tile_cols = ice.shape
    chunks = tile_cols // LANES
    table = jnp.asarray(weld_table())
    vmem = pl.BlockSpec(memory_space=pltpu.VMEM)
    block = pl.BlockSpec((NFSD, tile_rows, tile_cols), lambda n: (n, 0, 0))
    return pl.pallas_call(
        functools.partial(step_kernel, blk_count, lat_count, cells),
        grid=(planes // NFSD,),
        out_shape=jax.ShapeDtypeStruct(ice.shape, jnp.float32),
        in_specs=[pl.BlockSpec(memory_space=pltpu.SMEM), block] + [vmem] * 6,
        out_specs=block,
        scratch_shapes=[
            pltpu.VMEM((3, NFSD * chunks * EXT, LANES), jnp.float32),
            pltpu.VMEM((9, tile_rows, tile_cols), jnp.float32),
            pltpu.VMEM((tile_rows, tile_cols), jnp.float32),
            pltpu.VMEM((tile_rows, tile_cols), jnp.float32),
            pltpu.VMEM((2, 3, chunks, 64, LANES), jnp.float32),
            pltpu.VMEM((2, tile_rows, LANES), jnp.float32),
            pltpu.VMEM((NFSD * SUB, 2 * LANES), jnp.float32),
        ],
        compiler_params=pltpu.CompilerParams(vmem_limit_bytes=40 * 1024 * 1024),
        name="advance",
    )(cover, ice, weights, weld, received, rows_a, rows_b, table)


def on_device(ice_area, departure_weights, weld_rate, ice_cover, wave_ocean, ocean_route):
    cat_count, floe_count, tile_rows, tile_cols = ice_area.shape
    lat_count = lax.axis_size("lat")
    blk_count = lax.axis_size("blk")
    cells = wave_ocean.shape[3]
    dests = wave_ocean.shape[2]
    ice = ice_area.reshape(cat_count * floe_count, tile_rows, tile_cols)
    message, rows_a, rows_b = pack(ice, wave_ocean[0], ocean_route, blk_count, lat_count)
    received = lax.all_to_all(message, AXES, split_axis=0, concat_axis=0, tiled=True)

    pairs_a, pairs_b = [], []
    for b in range(blk_count):
        for l in range(lat_count):
            here = b * lat_count + l
            pairs_a.append((here, here ^ 1 if lat_count % 2 == 0 else here))
            if l == lat_count - 1:
                pairs_b.append((here, (blk_count - 1 - b) * lat_count + l))
            elif l > 0:
                pairs_b.append((here, here + 1 if l % 2 else here - 1))
    from_a = lax.ppermute(rows_a, AXES, pairs_a)
    from_b = lax.ppermute(rows_b, AXES, pairs_b)
    result = advance(
        ice_cover.reshape(1, tile_rows), ice, departure_weights, weld_rate,
        received.reshape(dests * PITCH, LANES), from_a, from_b, blk_count, lat_count, cells,
    )
    return result.reshape(ice_area.shape)


def solution(mesh):
    return jax.shard_map(
        on_device,
        mesh=mesh,
        in_specs=(
            P(None, None, "lat", "blk"),
            P(None, "lat", "blk"),
            P("lat", "blk"),
            P("lat", "blk"),
            P(("blk", "lat"), None, None, None),
            P(("blk", "lat"), None),
        ),
        out_specs=P(None, None, "lat", "blk"),
        check_vma=False,
    )
```

profile of v0, /device:TPU:0, one launch (start us, length us, event | category | flops | bytes accessed | tf_op | source)
XLA Modules:
  0.0 72.3 jit_solution(15565617440515247908)
XLA Ops:
  0.0 0.0 copy-start.7
  0.0 0.0 copy-start
  0.0 3.2 %copy-done = f32[5,12,32,1024]{3,2,1,0:T(8,128)S(1)} copy-done((f32[5,12,32,1024]{3,2,1,0:T(8,128)S(1)}, f32[5,12,32,1024]{3,2,1,0:T(8,128)}, u32[]{:S(2)}) %copy-start) | copy-done | bytes 7864344
  3.2 0.0 copy-start.2
  3.3 1.9 %copy-done.2 = f32[1,25,32,1024]{3,2,1,0:T(8,128)S(1)} copy-done((f32[1,25,32,1024]{3,2,1,0:T(8,128)S(1)}, f32[1,25,32,1024]{3,2,1,0:T(8,128)}, u32[]{:S(2)}) %copy-start.2) | copy-done | bytes 3276824
  5.2 0.0 copy-start.6
  5.2 0.7 copy-done.6
  5.8 0.0 copy-start.3
  5.8 0.0 copy-start.4
  5.8 0.0 copy-start.5
  5.8 6.6 %pack.1 = (f32[32,24,128]{2,1,0:T(8,128)}, f32[8,64,128]{2,1,0:T(8,128)S(1)}, f32[8,64,128]{2,1,0:T(8,128)S(1)}) custom-call(f32[25,32,1024]{2,1,0:T(8,128)S(1)} %bitcast.7, f32[60,32,1024]{2,1,0:T(8,128)S(1)} %bitcast.5, s32[1,32]{1,0:T(1,128)S(1)} %copy-done.6), custom_call_target="tpu_custom_call" | custom-call | tf_op jit(solution)/shard_map/pack/pallas_call | solution.py:135
  12.5 7.3 %all-to-all-start = ((f32[32,24,128]{2,1,0:T(8,128)}), f32[32,24,128]{2,1,0:T(8,128)S(1)}, u32[]{:S(2)}, u32[]{:S(2)}) async-start(f32[32,24,128]{2,1,0:T(8,128)} %get-tuple-element.8), calls=%async_computation | async-start | bytes 786432 | tf_op jit(solution)/shard_map/all_to_all | solution.py:387
  19.8 0.3 collective-permute-start
  20.1 0.7 collective-permute-start.1
  20.8 0.6 collective-permute-done.rows_a
  21.4 0.0 collective-permute-done.1.rows_b
  21.4 14.4 %all-to-all-done = f32[32,24,128]{2,1,0:T(8,128)S(1)} async-done(((f32[32,24,128]{2,1,0:T(8,128)}), f32[32,24,128]{2,1,0:T(8,128)S(1)}, u32[]{:S(2)}, u32[]{:S(2)}) %all-to-all-start) | async-done | bytes 393248 | tf_op jit(solution)/shard_map/all_to_all | solution.py:387
  35.8 0.0 copy-done.7
  35.8 0.0 copy-done.3
  35.8 0.0 copy-done.4
  35.8 0.0 copy-done.5
  35.8 0.0 copy-start.1
  35.8 3.2 %copy-done.1 = f32[5,12,32,1024]{3,2,1,0:T(8,128)S(1)} copy-done((f32[5,12,32,1024]{3,2,1,0:T(8,128)S(1)}, f32[5,12,32,1024]{3,2,1,0:T(8,128)}, u32[]{:S(2)}) %copy-start.1) | copy-done | bytes 7864344
  39.0 33.3 %advance.1 = f32[60,32,1024]{2,1,0:T(8,128)} custom-call(s32[1,32]{1,0:T(1,128)S(1)} %bitcast.9, f32[60,32,1024]{2,1,0:T(8,128)S(1)} %bitcast.6, s32[9,32,1024]{2,1,0:T(8,128)S(1)} %copy-done.3, f32[32,1024]{1,0:T(8,128)S(1)} %copy-done.4, f32[768,128]{1,0:T(8,128)S(1)} %bitcast.8, f32[8,64,128]{2,1,0:T(8,128)S(1)} %collective-permute-done.rows_a, ...), custom_call_target="tpu_custom_call" | custom-call | tf_op jit(solution)/shard_map/advance/pallas_call | solution.py:359
Async XLA Ops:
  0.0 35.8 %copy-start.7 = (s32[32,1]{0,1:T(1,128)S(1)}, s32[32,1]{0,1:T(1,128)}, u32[]{:S(2)}) copy-start(s32[32,1]{0,1:T(1,128)} %param.10) | copy-start | bytes 388
  0.0 3.2 %copy-start = (f32[5,12,32,1024]{3,2,1,0:T(8,128)S(1)}, f32[5,12,32,1024]{3,2,1,0:T(8,128)}, u32[]{:S(2)}) copy-start(f32[5,12,32,1024]{3,2,1,0:T(8,128)} %param.7) | copy-start | bytes 23592964
  3.2 1.9 %copy-start.2 = (f32[1,25,32,1024]{3,2,1,0:T(8,128)S(1)}, f32[1,25,32,1024]{3,2,1,0:T(8,128)}, u32[]{:S(2)}) copy-start(f32[1,25,32,1024]{3,2,1,0:T(8,128)} %param.11) | copy-start | bytes 9830404
  5.2 0.7 copy-start.6
  5.8 29.9 %copy-start.3 = (s32[9,32,1024]{2,1,0:T(8,128)S(1)}, s32[9,32,1024]{2,1,0:T(8,128)}, u32[]{:S(2)}) copy-start(s32[9,32,1024]{2,1,0:T(8,128)} %weights.1) | copy-start | bytes 3538948
  5.8 29.9 %copy-start.4 = (f32[32,1024]{1,0:T(8,128)S(1)}, f32[32,1024]{1,0:T(8,128)}, u32[]{:S(2)}) copy-start(f32[32,1024]{1,0:T(8,128)} %weld.1) | copy-start | bytes 393220
  5.8 29.9 %copy-start.5 = (bf16[96,256]{1,0:T(8,128)(2,1)S(1)}, bf16[96,256]{1,0:T(8,128)(2,1)}, u32[]{:S(2)}) copy-start(bf16[96,256]{1,0:T(8,128)(2,1)} %constant.2.clone.table) | copy-start | bytes 147460
  12.5 23.3 %all-to-all-start = ((f32[32,24,128]{2,1,0:T(8,128)}), f32[32,24,128]{2,1,0:T(8,128)S(1)}, u32[]{:S(2)}, u32[]{:S(2)}) async-start(f32[32,24,128]{2,1,0:T(8,128)} %get-tuple-element.8), calls=%async_computation | async-start | bytes 786432 | tf_op jit(solution)/shard_map/all_to_all | solution.py:387
  19.8 1.6 %collective-permute-start = (f32[8,64,128]{2,1,0:T(8,128)S(1)}, f32[8,64,128]{2,1,0:T(8,128)S(1)}, u32[]{:S(2)}, u32[]{:S(2)}) collective-permute-start(f32[8,64,128]{2,1,0:T(8,128)S(1)} %get-tuple-element.9), channel_id=1, source_target_pairs={{0,1},{1,0},{2,3},{3,2},{4,5},{5,4},{6,7},{7,6},{8,9},{9,8},{10,11... | collective-permute-start | bytes 786440 | tf_op jit(solution)/shard_map/ppermute | solution.py:398
  20.1 1.3 %collective-permute-start.1 = (f32[8,64,128]{2,1,0:T(8,128)S(1)}, f32[8,64,128]{2,1,0:T(8,128)S(1)}, u32[]{:S(2)}, u32[]{:S(2)}) collective-permute-start(f32[8,64,128]{2,1,0:T(8,128)S(1)} %get-tuple-element.10), channel_id=1, source_target_pairs={{1,2},{2,1},{3,4},{4,3},{5,6},{6,5},{7,31},{9,10},{10,9},{11,12},{... | collective-permute-start | bytes 786440 | tf_op jit(solution)/shard_map/ppermute | solution.py:399
  35.8 3.2 %copy-start.1 = (f32[5,12,32,1024]{3,2,1,0:T(8,128)S(1)}, f32[5,12,32,1024]{3,2,1,0:T(8,128)}, u32[]{:S(2)}) copy-start(f32[5,12,32,1024]{3,2,1,0:T(8,128)} %param.7) | copy-start | bytes 23592964
where the time goes:
time: 72.6 us; the launch traced here: 72.3 us
  Pallas kernels  39.9 us (55%)
  waiting for transfers between devices  15 us (21%)
  local copies, waits for them, and re-layouts  9.07 us (12%)
  starting transfers between devices  8.29 us (11%)
    pallas_call x1, Pallas kernels, advance(): pl.pallas_call(functools.partial(step_kernel, blk_count, lat_count, cells...  33.3 us
    all_to_all x1, waiting for transfers between devices, on_device(): lax.all_to_all(message, AXES, split_axis=0, concat_axis=0, tiled=True)  14.4 us
    unnamed x16, local copies, waits for them, and re-layouts  9.07 us
    all_to_all x1, starting transfers between devices, on_device(): lax.all_to_all(message, AXES, split_axis=0, concat_axis=0, tiled=True)  7.3 us
    pallas_call x1, Pallas kernels, pack(): pl.pallas_call(functools.partial(pack_kernel, blk_count, lat_count), out_...  6.62 us
  transfers between devices with their start and end apart: 3, of which 2 were waited for; matrix products, arithmetic and copies ran while one was open for 0% of the time, Pallas kernels for 0%

commit v1 on v0

v1 whole, which is shorter than its diff:
```python
import functools

import jax
import jax.numpy as jnp
import ml_dtypes
import numpy as np
from jax import lax
from jax.experimental import pallas as pl
from jax.experimental.pallas import tpu as pltpu
from jax.sharding import PartitionSpec as P

NCAT = 5
NFSD = 12
FREQ = 25
PLANES = NCAT * NFSD
LANES = 128
SUB = 8
EXT = 41
VMEM_LIMIT = 56 * 1024 * 1024
AXES = ("blk", "lat")

fracture_step = 0.1
weld_scale = 840.0 / 1024.0


def weld_table():
    index = np.arange(NFSD)
    apart = index[:, None] - index[None, :]
    exact = np.where(apart > 0, 1.0, -1.0) / (1.0 + np.abs(apart)) * weld_scale
    high = exact.astype(ml_dtypes.bfloat16).astype(np.float64)
    low = exact - high
    kept = [0, 1, 2, 3, 8, 9, 10, 11]
    assert not np.delete(low, kept, axis=1).any()
    joined = np.concatenate([high, high, low[:, kept]], axis=1)
    return np.kron(joined, np.eye(SUB)).astype(ml_dtypes.bfloat16)


def pack_kernel(
    blk_count, lat_count, wave, ice, route, message, rows_a, rows_b, to_west, to_east,
    wave_buf, west_buf, east_buf, sums, corners, wave_sem, col_sem, row_sem,
):
    freq_count, dests, cells = wave.shape
    planes, tile_rows, tile_cols = ice.shape
    chunks = tile_cols // LANES
    bands = tile_rows // SUB
    me_b = lax.axis_index("blk")
    me_l = lax.axis_index("lat")

    col_copies, wave_copies = [], []
    for p in range(NCAT):
        own = pl.ds(p * NFSD, NFSD)
        for side, (buf, start) in enumerate(((west_buf, 0), (east_buf, tile_cols - LANES))):
            col_copies.append(
                pltpu.make_async_copy(
                    ice.at[own, :, pl.ds(start, LANES)], buf.at[own], col_sem.at[side, p]
                )
            )
    groups = wave_sem.shape[0]
    step = dests // groups
    for p in range(groups):
        own = pl.ds(p * step, step)
        wave_copies.append(
            pltpu.make_async_copy(wave.at[:, own, :], wave_buf.at[:, own, :], wave_sem.at[p])
        )
    odd = lax.rem(me_l, 2) == 1
    first = jnp.where(odd, 0, tile_rows - 1)
    second = jnp.where(odd, tile_rows - 1, 0)
    row_copies = []
    for j in range(chunks):
        for which, (row, out) in enumerate(((first, rows_a), (second, rows_b))):
            row_copies.append(
                pltpu.make_async_copy(
                    ice.at[:, row, pl.ds(j * LANES, LANES)],
                    out.at[j, pl.ds(0, planes), :],
                    row_sem.at[which, j],
                )
            )
    for copy in col_copies + wave_copies + row_copies:
        copy.start()

    lane = lax.broadcasted_iota(jnp.int32, (SUB, LANES), 1)
    columns = [jnp.zeros((SUB, LANES), jnp.float32) for _ in range(2 * bands)]
    for p in range(planes):
        if p % NFSD == 0:
            for copy in col_copies[2 * (p // NFSD) : 2 * (p // NFSD) + 2]:
                copy.wait()
        for i in range(bands):
            band = slice(SUB * i, SUB * i + SUB)
            ends = jnp.where(lane == 0, west_buf[p, band, :], east_buf[p, band, :])
            ends = pltpu.roll(ends, p, 1) if p else ends
            columns[i] = jnp.where(lane == p, ends, columns[i])
            columns[bands + i] = jnp.where(lane == (p - 1) % LANES, ends, columns[bands + i])
    east = [pltpu.roll(part, 1, 1) for part in columns[bands:]]
    for side, (parts_of, out) in enumerate(((columns[:bands], to_west), (east, to_east))):
        for i in range(bands // 2):
            out[SUB * i : SUB * i + SUB, :] = jnp.where(
                lane < 64, parts_of[i], pltpu.roll(parts_of[bands // 2 + i], 64, 1)
            )
        corners[2 * side : 2 * side + 1, :] = parts_of[0][0:1, :]
        corners[2 * side + 1 : 2 * side + 2, :] = parts_of[bands - 1][SUB - 1 : SUB, :]

    for group in range(dests // SUB):
        band = slice(SUB * group, SUB * group + SUB)
        if group * SUB % step == 0:
            wave_copies[group * SUB // step].wait()
        for j in range(cells // LANES):
            chunk = slice(LANES * j, LANES * j + LANES)
            total = wave_buf[0, band, chunk] * np.float32(1.0 / freq_count)
            for f in range(1, freq_count):
                total = total + wave_buf[f, band, chunk] * np.float32((f + 1.0) / freq_count)
            sums[j, band, :] = total

    side_of = []
    for to_b in range(blk_count):
        last_col = (to_b == lax.rem(me_b + 1, blk_count)) | (
            to_b == lax.rem(2 * blk_count - 2 - me_b, blk_count)
        )
        side_of.append(jnp.where(last_col, 2, 0))
    row_of = [jnp.where(to_l < me_l, 0, 1) for to_l in range(lat_count)]
    for m in range(dests):
        to = route[0, m]
        for j in range(cells // LANES):
            message[to, :, LANES * j : LANES * j + LANES] = sums[j, m : m + 1, :]
        which = side_of[m // lat_count] + row_of[m % lat_count]
        message[m, :, cells : cells + LANES] = corners[pl.ds(which, 1), :]
    for copy in row_copies:
        copy.wait()


def pack(ice, wave, route, blk_count, lat_count):
    planes, tile_rows, tile_cols = ice.shape
    freq_count, dests, cells = wave.shape
    chunks = tile_cols // LANES
    hbm = pl.BlockSpec(memory_space=pl.ANY)
    vmem = pl.BlockSpec(memory_space=pltpu.VMEM)
    rows = jax.ShapeDtypeStruct((chunks, 64, LANES), jnp.float32)
    column = jax.ShapeDtypeStruct((tile_rows // 2, LANES), jnp.float32)
    return pl.pallas_call(
        functools.partial(pack_kernel, blk_count, lat_count),
        out_shape=(
            jax.ShapeDtypeStruct((dests, 1, cells + LANES), jnp.float32),
            rows, rows, column, column,
        ),
        in_specs=[hbm, hbm, pl.BlockSpec(memory_space=pltpu.SMEM)],
        out_specs=(vmem,) * 5,
        scratch_shapes=[
            pltpu.VMEM((freq_count, dests, cells), jnp.float32),
            pltpu.VMEM((planes, tile_rows, LANES), jnp.float32),
            pltpu.VMEM((planes, tile_rows, LANES), jnp.float32),
            pltpu.VMEM((cells // LANES, dests, LANES), jnp.float32),
            pltpu.VMEM((SUB, LANES), jnp.float32),
            pltpu.SemaphoreType.DMA((4,)),
            pltpu.SemaphoreType.DMA((2, NCAT)),
            pltpu.SemaphoreType.DMA((2, chunks)),
        ],
        compiler_params=pltpu.CompilerParams(vmem_limit_bytes=VMEM_LIMIT),
        name="pack",
    )(wave, ice, route)


def step_kernel(
    blk_count, lat_count, cells,
    cover, ice, weights, weld, received, rows_a, rows_b, west_col, east_col, table, out,
    ice_buf, out_buf, weight_buf, ext_even, ext_odd, scaled, weld_now, rate, ghosts, cols,
    moved_even, moved_odd, stacked_even, stacked_odd, exchange_table, ice_sem, weight_sem, out_sem,
):
    tile_rows, tile_cols = weld.shape
    bands = tile_rows // SUB
    chunks = tile_cols // LANES
    plane_pitch = chunks * EXT + 1
    lane = lax.broadcasted_iota(jnp.int32, (SUB, LANES), 1)
    sublane = lax.broadcasted_iota(jnp.int32, (SUB, LANES), 0)
    me_b = lax.axis_index("blk")
    me_l = lax.axis_index("lat")
    exts = (ext_even, ext_odd)
    moveds = (moved_even, moved_odd)
    stackeds = (stacked_even, stacked_odd)

    def category(n):
        return pl.ds(n * NFSD, NFSD)

    ice_copies = [
        pltpu.make_async_copy(ice.at[category(n)], ice_buf.at[category(n)], ice_sem.at[n])
        for n in range(NCAT)
    ]
    weight_copy = pltpu.make_async_copy(weights, weight_buf, weight_sem)
    out_copies = [
        pltpu.make_async_copy(out_buf.at[category(n)], out.at[category(n)], out_sem.at[n])
        for n in range(NCAT)
    ]
    ice_copies[0].start()
    weight_copy.start()
    for copy in ice_copies[1:]:
        copy.start()

    def shifted(pieces, west, east):
        to_right = [pltpu.roll(piece, 1, 1) for piece in pieces]
        to_left = [pltpu.roll(piece, LANES - 1, 1) for piece in pieces]
        from_west = [
            jnp.where(lane == 0, to_right[j - 1] if j else west, to_right[j])
            for j in range(chunks)
        ]
        from_east = [
            jnp.where(lane == LANES - 1, to_left[j + 1] if j + 1 < chunks else east, to_left[j])
            for j in range(chunks)
        ]
        return from_west, pieces, from_east

    top = me_l == lat_count - 1
    bottom = me_l == 0
    odd = lax.rem(me_l, 2) == 1
    west_b = lax.rem(me_b + blk_count - 1, blk_count)
    east_b = lax.rem(me_b + 1, blk_count)
    above_l = jnp.minimum(me_l + 1, lat_count - 1)
    below_l = jnp.maximum(me_l - 1, 0)

    half = tile_rows // 2
    for side, column in enumerate((west_col, east_col)):
        for i in range(bands // 2):
            packed = column[SUB * i : SUB * i + SUB, :]
            cols[side, SUB * i : SUB * i + SUB, :] = packed
            cols[side, half + SUB * i : half + SUB * i + SUB, :] = pltpu.roll(packed, 64, 1)

    def corner(b, l):
        line = received[b * lat_count + l, :, cells : cells + LANES]
        spread = jnp.broadcast_to(line, (SUB, LANES))
        return [
            jnp.sum(jnp.where(lane == SUB * q + sublane, spread, 0.0), axis=1, keepdims=True)
            for q in range(SUB)
        ]

    below_corners = [corner(b, below_l) for b in (west_b, east_b)]
    above_corners = [
        corner(jnp.where(top, fold_b, b), above_l)
        for fold_b, b in (
            (lax.rem(blk_count - me_b, blk_count), west_b),
            (lax.rem(2 * blk_count - 2 - me_b, blk_count), east_b),
        )
    ]
    backwards = LANES - 1 - lane
    for q in range(SUB):
        band = pl.ds(SUB * q, SUB)
        below = [
            jnp.where(bottom, 0.0, jnp.where(odd, rows_a[j, band, :], rows_b[j, band, :]))
            for j in range(chunks)
        ]
        above = [jnp.where(odd, rows_b[j, band, :], rows_a[j, band, :]) for j in range(chunks)]
        folded = [
            jnp.take_along_axis(above[chunks - 1 - j], backwards, axis=1) for j in range(chunks)
        ]
        above = [jnp.where(top, folded[j], above[j]) for j in range(chunks)]
        for side, (pieces, corners) in enumerate(((below, below_corners), (above, above_corners))):
            ends = [jnp.broadcast_to(corners[s][q], (SUB, LANES)) for s in range(2)]
            if side == 0:
                ends = [jnp.where(bottom, 0.0, end) for end in ends]
            for dx, line in enumerate(shifted(pieces, *ends)):
                for j in range(chunks):
                    ghosts[side, dx, j, band, :] = line[j]

    per_row = tile_cols // cells
    for r in range(tile_rows):
        for j in range(chunks):
            o = r * per_row + j * LANES // cells
            start = j * LANES % cells
            rate[r : r + 1, LANES * j : LANES * j + LANES] = received[o, :, start : start + LANES]
    for i in range(bands):
        mask = jnp.zeros((SUB, LANES), jnp.float32)
        for r in range(SUB):
            here = (cover[0, SUB * i + r] > 0).astype(jnp.float32)
            mask = jnp.where(sublane == r, here, mask)
        for j in range(chunks):
            own = (slice(SUB * i, SUB * i + SUB), slice(LANES * j, LANES * j + LANES))
            rate[own] = rate[own] * (mask * np.float32(fracture_step / 11.0))
            weld_now[own] = weld[own] * mask * np.float32(0.06 / weld_scale)

    def border(n):
        ext = exts[n % 2]
        for side in range(2):
            row = 7 if side == 0 else 8 + tile_rows
            for dx in range(3):
                for j in range(chunks):
                    for k0 in (0, NFSD - SUB):
                        start = k0 * plane_pitch + j * EXT + row
                        ext[dx, pl.ds(start, SUB, stride=plane_pitch), :] = ghosts[
                            side, dx, j, pl.ds(n * NFSD + k0, SUB), :
                        ]

    def widen(n, unit):
        ext = exts[n % 2]
        i = unit // NFSD
        k = unit - i * NFSD
        p = n * NFSD + k
        rows = pl.ds(pl.multiple_of(i * SUB, SUB), SUB)
        pieces = [ice_buf[p, rows, LANES * j : LANES * j + LANES] for j in range(chunks)]
        west = pltpu.roll(cols[0, rows, :], LANES - p, 1)
        east = pltpu.roll(cols[1, rows, :], LANES - 1 - p, 1)
        for dx, line in enumerate(shifted(pieces, west, east)):
            for j in range(chunks):
                ext[dx, pl.ds(k * plane_pitch + j * EXT + SUB + i * SUB, SUB), :] = line[j]

    width = 2
    span = LANES * width
    per_band = chunks // width
    tiles = bands * per_band

    def place(t):
        return t // per_band, lax.rem(t, per_band)

    def stencil(n, t, slot):
        ext, moved, stacked = exts[n % 2], moveds[slot], stackeds[slot]
        i, jj = place(t)
        rows = pl.ds(pl.multiple_of(i * SUB, SUB), SUB)
        for s in range(width):
            j = jj * width + s
            columns = pl.ds(pl.multiple_of(j * LANES, LANES), LANES)
            factors = [scaled[w, rows, columns] for w in range(9)]
            base = j * EXT + i * SUB + 7
            for k in range(NFSD):
                total = None
                for w in range(9):
                    dy, dx = w // 3, w % 3
                    term = factors[w] * ext[dx, pl.ds(base + k * plane_pitch + dy, SUB), :]
                    total = term if total is None else total + term
                moved[SUB * k : SUB * k + SUB, LANES * s : LANES * s + LANES] = total
        whole = moved[...]
        high = whole.astype(jnp.bfloat16)
        low = (whole - high.astype(jnp.float32)).astype(jnp.bfloat16)
        stacked[...] = jnp.concatenate([high, low, high[: 4 * SUB], high[8 * SUB :]], axis=0)

    def exchange_of(slot):
        return jnp.dot(exchange_table[...], stackeds[slot][...], preferred_element_type=jnp.float32)

    def finish(n, t, slot, exchange):
        moved = moveds[slot]
        i, jj = place(t)
        rows = pl.ds(pl.multiple_of(i * SUB, SUB), SUB)
        columns = pl.ds(pl.multiple_of(jj * span, span), span)
        speed = weld_now[rows, columns]
        breaking = rate[rows, columns] * np.float32(1.0 / (1.0 + 0.5 * n))
        own = [moved[SUB * k : SUB * k + SUB, :] for k in range(NFSD)]
        squares = [area * (area * np.float32(weld_scale)) for area in own]
        welded = []
        for k in range(NFSD):
            turn = own[k] * exchange[SUB * k : SUB * k + SUB, :]
            if k:
                turn = turn + squares[k - 1]
            if k == NFSD - 1:
                turn = turn + squares[k]
            welded.append(own[k] + speed * turn)
        carried = None
        for k in range(NFSD - 1, -1, -1):
            if k:
                broken = breaking * welded[k]
                change = broken * np.float32(-k)
                if carried is not None:
                    change = carried + change
                carried = broken if carried is None else carried + broken
            else:
                change = carried
            out_buf[n * NFSD + k, rows, columns] = welded[k] + change

    per_tile = bands * NFSD // tiles

    def pair(n, t, last):
        more = n + 1 < NCAT
        for s in range(2):
            exchange = exchange_of(s)
            if last and s == 1:
                if more:
                    for u in range(per_tile):
                        widen(n + 1, (t + s) * per_tile + u)
                    stencil(n + 1, 0, 0)
                finish(n, t + s, s, exchange)
            else:
                stencil(n, t + s + 1, 1 - s)
                finish(n, t + s, s, exchange)
                if more:
                    for u in range(per_tile):
                        widen(n + 1, (t + s) * per_tile + u)

    exchange_table[...] = table[...].astype(jnp.bfloat16)
    weight_copy.wait()
    for w in range(9):
        scaled[w] = weight_buf[w].astype(jnp.float32) * np.float32(1.0 / 4096.0)
    ice_copies[0].wait()
    border(0)

    def first_units(u, _):
        widen(0, u)
        return 0

    lax.fori_loop(0, bands * NFSD, first_units, 0, unroll=2)
    stencil(0, 0, 0)
    for n in range(NCAT):
        if n + 1 < NCAT:
            ice_copies[n + 1].wait()
            border(n + 1)

        def both(h, _):
            pair(n, h * 2, False)
            return 0

        lax.fori_loop(0, tiles // 2 - 1, both, 0)
        pair(n, tiles - 2, True)
        out_copies[n].start()
    for copy in out_copies:
        copy.wait()


def advance(
    cover, ice, weights, weld, received, rows_a, rows_b, west_col, east_col,
    blk_count, lat_count, cells,
):
    planes, tile_rows, tile_cols = ice.shape
    chunks = tile_cols // LANES
    table = jnp.asarray(weld_table().astype(np.float32))
    vmem = pl.BlockSpec(memory_space=pltpu.VMEM)
    hbm = pl.BlockSpec(memory_space=pl.ANY)
    tile = pltpu.VMEM((tile_rows, tile_cols), jnp.float32)
    ext = pltpu.VMEM((3, NFSD * (chunks * EXT + 1), LANES), jnp.float32)
    moved = pltpu.VMEM((NFSD * SUB, 2 * LANES), jnp.float32)
    stacked = pltpu.VMEM((2 * LANES, 2 * LANES), jnp.bfloat16)
    return pl.pallas_call(
        functools.partial(step_kernel, blk_count, lat_count, cells),
        out_shape=jax.ShapeDtypeStruct(ice.shape, jnp.float32),
        in_specs=[pl.BlockSpec(memory_space=pltpu.SMEM), hbm, hbm] + [vmem] * 7,
        out_specs=hbm,
        scratch_shapes=[
            pltpu.VMEM(ice.shape, jnp.float32),
            pltpu.VMEM(ice.shape, jnp.float32),
            pltpu.VMEM(weights.shape, jnp.int32),
            ext, ext,
            pltpu.VMEM(weights.shape, jnp.float32),
            tile, tile,
            pltpu.VMEM((2, 3, chunks, 64, LANES), jnp.float32),
            pltpu.VMEM((2, tile_rows, LANES), jnp.float32),
            moved, moved, stacked, stacked,
            pltpu.VMEM((NFSD * SUB, 2 * LANES), jnp.bfloat16),
            pltpu.SemaphoreType.DMA((NCAT,)),
            pltpu.SemaphoreType.DMA,
            pltpu.SemaphoreType.DMA((NCAT,)),
        ],
        compiler_params=pltpu.CompilerParams(vmem_limit_bytes=VMEM_LIMIT),
        name="advance",
    )(cover, ice, weights, weld, received, rows_a, rows_b, west_col, east_col, table)


def on_device(ice_area, departure_weights, weld_rate, ice_cover, wave_ocean, ocean_route):
    cat_count, floe_count, tile_rows, tile_cols = ice_area.shape
    lat_count = lax.axis_size("lat")
    blk_count = lax.axis_size("blk")
    assert lat_count % 2 == 0 and blk_count % 2 == 0 and blk_count > 2
    cells = wave_ocean.shape[3]
    ice = ice_area.reshape(cat_count * floe_count, tile_rows, tile_cols)
    message, rows_a, rows_b, to_west, to_east = pack(
        ice, wave_ocean[0], ocean_route, blk_count, lat_count
    )
    received = lax.all_to_all(message, AXES, split_axis=0, concat_axis=0, tiled=True)

    pairs_a, pairs_b = [], []
    for b in range(blk_count):
        for l in range(lat_count):
            here = b * lat_count + l
            pairs_a.append((here, here ^ 1))
            if l == lat_count - 1:
                pairs_b.append((here, (blk_count - 1 - b) * lat_count + l))
            elif l > 0:
                pairs_b.append((here, here + 1 if l % 2 else here - 1))
    from_a = lax.ppermute(rows_a, AXES, pairs_a)
    from_b = lax.ppermute(rows_b, AXES, pairs_b)
    ring = [(b, (b + 1) % blk_count) for b in range(blk_count)]
    west_col = lax.ppermute(to_east, "blk", ring)
    east_col = lax.ppermute(to_west, "blk", [(b, a) for a, b in ring])
    result = advance(
        ice_cover.reshape(1, tile_rows), ice, departure_weights, weld_rate,
        received, from_a, from_b, west_col, east_col, blk_count, lat_count, cells,
    )
    return result.reshape(ice_area.shape)


def solution(mesh):
    return jax.shard_map(
        on_device,
        mesh=mesh,
        in_specs=(
            P(None, None, "lat", "blk"),
            P(None, "lat", "blk"),
            P("lat", "blk"),
            P("lat", "blk"),
            P(("blk", "lat"), None, None, None),
            P(("blk", "lat"), None),
        ),
        out_specs=P(None, None, "lat", "blk"),
        check_vma=False,
    )
```

time: 72.6 us -> 45.9 us (0.63)
  the two profiles are of different devices: /device:TPU:0 before, /device:TPU:3 now
where the time goes in v1:
time: 45.9 us; the launch traced here: 45.7 us
  Pallas kernels  26.7 us (58%)
  starting transfers between devices  13.3 us (29%)
  waiting for transfers between devices  4.87 us (11%)
  local copies, waits for them, and re-layouts  0.72 us (2%)
    pallas_call x1, Pallas kernels, advance(): pl.pallas_call(functools.partial(step_kernel, blk_count, lat_count, cells...  21.7 us
    all_to_all x1, starting transfers between devices, on_device(): lax.all_to_all(message, AXES, split_axis=0, concat_axis=0, tiled=True)  6.45 us
    pallas_call x1, Pallas kernels, pack(): pl.pallas_call(functools.partial(pack_kernel, blk_count, lat_count), out_...  4.99 us
    ppermute x1, waiting for transfers between devices, on_device(): from_b = lax.ppermute(rows_b, AXES, pairs_b)  3.61 us
    ppermute x1, starting transfers between devices, on_device(): from_b = lax.ppermute(rows_b, AXES, pairs_b)  3.11 us
    ppermute x1, starting transfers between devices, on_device(): east_col = lax.ppermute(to_west, 'blk', [(b, a) for a, b in ring])  2.08 us
    ppermute x1, waiting for transfers between devices, on_device(): west_col = lax.ppermute(to_east, 'blk', ring)  1.25 us
    ppermute x1, starting transfers between devices, on_device(): west_col = lax.ppermute(to_east, 'blk', ring)  1.24 us
  transfers between devices with their start and end apart: 5, of which 2 were waited for; matrix products, arithmetic and copies ran while one was open for 0% of the time, Pallas kernels for 0%

profile of v1, /device:TPU:3, one launch (start us, length us, event | category | flops | bytes accessed | tf_op | source)
XLA Modules:
  0.0 45.7 jit_solution(13173145615602262433)
XLA Ops:
  0.0 5.0 %pack.1 = (f32[32,1,1152]{2,1,0:T(1,128)}, f32[8,64,128]{2,1,0:T(8,128)}, f32[8,64,128]{2,1,0:T(8,128)}, f32[16,128]{1,0:T(8,128)}, f32[16,128]{1,0:T(8,128)}) custom-call(f32[25,32,1024]{2,1,0:T(8,128)} %bitcast.6, f32[60,32,1024]{2,1,0:T(8,128)} %bitcast.4, s32[1,32]{1,0:T(1,128)} %route.1), custom_call_target="tpu_custom_call" | custom-call | tf_op jit(solution)/shard_map/pack/pallas_call | solution.py:138
  5.0 6.4 %all-to-all-start = ((f32[32,1,1152]{2,1,0:T(1,128)}), f32[32,1,1152]{2,1,0:T(1,128)S(1)}, u32[]{:S(2)}, u32[]{:S(2)}) async-start(f32[32,1,1152]{2,1,0:T(1,128)} %get-tuple-element.10), calls=%async_computation | async-start | bytes 294912 | tf_op jit(solution)/shard_map/all_to_all | solution.py:458
  11.5 0.4 collective-permute-start
  11.9 3.1 %collective-permute-start.1 = (f32[8,64,128]{2,1,0:T(8,128)}, f32[8,64,128]{2,1,0:T(8,128)S(1)}, u32[]{:S(2)}, u32[]{:S(2)}) collective-permute-start(f32[8,64,128]{2,1,0:T(8,128)} %get-tuple-element.12), channel_id=1, source_target_pairs={{1,2},{2,1},{3,4},{4,3},{5,6},{6,5},{7,31},{9,10},{10,9},{11,12},{... | collective-permute-start | bytes 786440 | tf_op jit(solution)/shard_map/ppermute | solution.py:470
  15.0 1.2 %collective-permute-start.2 = (f32[16,128]{1,0:T(8,128)}, f32[16,128]{1,0:T(8,128)S(1)}, u32[]{:S(2)}, u32[]{:S(2)}) collective-permute-start(f32[16,128]{1,0:T(8,128)} %get-tuple-element.13), channel_id=1, source_target_pairs={{0,8},{8,16},{16,24},{24,0},{1,9},{9,17},{17,25},{25,1},{2,10},{10... | collective-permute-start | bytes 24584 | tf_op jit(solution)/shard_map/ppermute | solution.py:472
  16.2 2.1 %collective-permute-start.3 = (f32[16,128]{1,0:T(8,128)}, f32[16,128]{1,0:T(8,128)S(1)}, u32[]{:S(2)}, u32[]{:S(2)}) collective-permute-start(f32[16,128]{1,0:T(8,128)} %get-tuple-element.14), channel_id=1, source_target_pairs={{8,0},{16,8},{24,16},{0,24},{9,1},{17,9},{25,17},{1,25},{10,2},{18... | collective-permute-start | bytes 24584 | tf_op jit(solution)/shard_map/ppermute | solution.py:473
  18.3 1.2 %collective-permute-done.2.west_col = f32[16,128]{1,0:T(8,128)S(1)} collective-permute-done((f32[16,128]{1,0:T(8,128)}, f32[16,128]{1,0:T(8,128)S(1)}, u32[]{:S(2)}, u32[]{:S(2)}) %collective-permute-start.2) | collective-permute-done | bytes 8224 | tf_op jit(solution)/shard_map/ppermute | solution.py:472
  19.6 0.0 copy-start.3
  19.6 0.0 collective-permute-done.3.east_col
  19.6 0.0 copy-start.4
  19.6 0.0 collective-permute-done.rows_a
  19.6 0.0 copy-start.1
  19.6 3.6 %collective-permute-done.1.rows_b = f32[8,64,128]{2,1,0:T(8,128)S(1)} collective-permute-done((f32[8,64,128]{2,1,0:T(8,128)}, f32[8,64,128]{2,1,0:T(8,128)S(1)}, u32[]{:S(2)}, u32[]{:S(2)}) %collective-permute-start.1) | collective-permute-done | bytes 262176 | tf_op jit(solution)/shard_map/ppermute | solution.py:470
  23.2 0.0 copy-start.2
  23.2 0.0 all-to-all-done.received
  23.2 0.0 copy-start
  23.2 0.0 copy-done.3
  23.2 0.0 copy-done.4
  23.2 0.0 copy-done.1
  23.2 0.7 %copy-done.2 = f32[8,64,128]{2,1,0:T(8,128)} copy-done((f32[8,64,128]{2,1,0:T(8,128)}, f32[8,64,128]{2,1,0:T(8,128)S(1)}, u32[]{:S(2)}) %copy-start.2) | copy-done | bytes 262168
  23.9 0.0 copy-done
  23.9 21.7 %advance.1 = f32[60,32,1024]{2,1,0:T(8,128)} custom-call(s32[1,32]{1,0:T(1,128)} %bitcast.7, f32[60,32,1024]{2,1,0:T(8,128)} %bitcast.5, s32[9,32,1024]{2,1,0:T(8,128)} %weights.1, f32[32,1024]{1,0:T(8,128)} %weld.1, f32[32,1,1152]{2,1,0:T(1,128)} %copy-done, f32[8,64,128]{2,1,0:T(8,128)} %copy-done.1, f32[8,64,128]{2,1,0:T(8,128)} %copy-done.2, ...), custom_call_target="tpu_custom_call" | custom-call | tf_op jit(solution)/shard_map/advance/pallas_call | solution.py:423
Async XLA Ops:
  5.0 18.2 %all-to-all-start = ((f32[32,1,1152]{2,1,0:T(1,128)}), f32[32,1,1152]{2,1,0:T(1,128)S(1)}, u32[]{:S(2)}, u32[]{:S(2)}) async-start(f32[32,1,1152]{2,1,0:T(1,128)} %get-tuple-element.10), calls=%async_computation | async-start | bytes 294912 | tf_op jit(solution)/shard_map/all_to_all | solution.py:458
  11.5 8.1 %collective-permute-start = (f32[8,64,128]{2,1,0:T(8,128)}, f32[8,64,128]{2,1,0:T(8,128)S(1)}, u32[]{:S(2)}, u32[]{:S(2)}) collective-permute-start(f32[8,64,128]{2,1,0:T(8,128)} %get-tuple-element.11), channel_id=1, source_target_pairs={{0,1},{1,0},{2,3},{3,2},{4,5},{5,4},{6,7},{7,6},{8,9},{9,8},{10,11... | collective-permute-start | bytes 786440 | tf_op jit(solution)/shard_map/ppermute | solution.py:469
  11.9 11.3 %collective-permute-start.1 = (f32[8,64,128]{2,1,0:T(8,128)}, f32[8,64,128]{2,1,0:T(8,128)S(1)}, u32[]{:S(2)}, u32[]{:S(2)}) collective-permute-start(f32[8,64,128]{2,1,0:T(8,128)} %get-tuple-element.12), channel_id=1, source_target_pairs={{1,2},{2,1},{3,4},{4,3},{5,6},{6,5},{7,31},{9,10},{10,9},{11,12},{... | collective-permute-start | bytes 786440 | tf_op jit(solution)/shard_map/ppermute | solution.py:470
  15.0 4.6 %collective-permute-start.2 = (f32[16,128]{1,0:T(8,128)}, f32[16,128]{1,0:T(8,128)S(1)}, u32[]{:S(2)}, u32[]{:S(2)}) collective-permute-start(f32[16,128]{1,0:T(8,128)} %get-tuple-element.13), channel_id=1, source_target_pairs={{0,8},{8,16},{16,24},{24,0},{1,9},{9,17},{17,25},{25,1},{2,10},{10... | collective-permute-start | bytes 24584 | tf_op jit(solution)/shard_map/ppermute | solution.py:472
  16.2 3.3 %collective-permute-start.3 = (f32[16,128]{1,0:T(8,128)}, f32[16,128]{1,0:T(8,128)S(1)}, u32[]{:S(2)}, u32[]{:S(2)}) collective-permute-start(f32[16,128]{1,0:T(8,128)} %get-tuple-element.14), channel_id=1, source_target_pairs={{8,0},{16,8},{24,16},{0,24},{9,1},{17,9},{25,17},{1,25},{10,2},{18... | collective-permute-start | bytes 24584 | tf_op jit(solution)/shard_map/ppermute | solution.py:473
  19.6 3.6 %copy-start.3 = (f32[16,128]{1,0:T(8,128)}, f32[16,128]{1,0:T(8,128)S(1)}, u32[]{:S(2)}) copy-start(f32[16,128]{1,0:T(8,128)S(1)} %collective-permute-done.2.west_col) | copy-start | bytes 24580
  19.6 3.6 %copy-start.4 = (f32[16,128]{1,0:T(8,128)}, f32[16,128]{1,0:T(8,128)S(1)}, u32[]{:S(2)}) copy-start(f32[16,128]{1,0:T(8,128)S(1)} %collective-permute-done.3.east_col) | copy-start | bytes 24580
  19.6 3.6 %copy-start.1 = (f32[8,64,128]{2,1,0:T(8,128)}, f32[8,64,128]{2,1,0:T(8,128)S(1)}, u32[]{:S(2)}) copy-start(f32[8,64,128]{2,1,0:T(8,128)S(1)} %collective-permute-done.rows_a) | copy-start | bytes 786436
  23.2 0.7 %copy-start.2 = (f32[8,64,128]{2,1,0:T(8,128)}, f32[8,64,128]{2,1,0:T(8,128)S(1)}, u32[]{:S(2)}) copy-start(f32[8,64,128]{2,1,0:T(8,128)S(1)} %collective-permute-done.1.rows_b) | copy-start | bytes 786436
  23.2 0.7 %copy-start = (f32[32,1,1152]{2,1,0:T(1,128)}, f32[32,1,1152]{2,1,0:T(1,128)S(1)}, u32[]{:S(2)}) copy-start(f32[32,1,1152]{2,1,0:T(1,128)S(1)} %all-to-all-done.received) | copy-start | bytes 442372

commit v2 on v1

--- a/solution.py
+++ b/solution.py
@@ -35,69 +35,90 @@
     return np.kron(joined, np.eye(SUB)).astype(ml_dtypes.bfloat16)
 
 
-def pack_kernel(
-    blk_count, lat_count, wave, ice, route, message, rows_a, rows_b, to_west, to_east,
-    wave_buf, west_buf, east_buf, sums, corners, wave_sem, col_sem, row_sem,
+def gather_edges(west_buf, east_buf, copies, planes, bands_of):
+    lane = lax.broadcasted_iota(jnp.int32, (SUB, LANES), 1)
+    west = [jnp.zeros((SUB, LANES), jnp.float32) for _ in bands_of]
+    east = list(west)
+    for p in range(planes):
+        if p % NFSD == 0:
+            for copy in copies[p // NFSD]:
+                copy.wait()
+        for i, start in enumerate(bands_of):
+            band = slice(start, start + SUB)
+            ends = jnp.where(lane == 0, west_buf[p, band, :], east_buf[p, band, :])
+            ends = pltpu.roll(ends, p, 1) if p else ends
+            west[i] = jnp.where(lane == p, ends, west[i])
+            east[i] = jnp.where(lane == (p - 1) % LANES, ends, east[i])
+    return west, [pltpu.roll(part, 1, 1) for part in east]
+
+
+def wave_kernel(
+    blk_count, lat_count, wave, ice, route_hbm, message, rows_a, rows_b,
+    edge_rows, route, wave_buf, west_buf, east_buf, sums, corners, route_sem, wave_sem, col_sem, row_sem, send_sem,
 ):
     freq_count, dests, cells = wave.shape
     planes, tile_rows, tile_cols = ice.shape
-    chunks = tile_cols // LANES
-    bands = tile_rows // SUB
     me_b = lax.axis_index("blk")
     me_l = lax.axis_index("lat")
 
-    col_copies, wave_copies = [], []
+    odd = lax.rem(me_l, 2) == 1
+    first = jnp.where(odd, 0, tile_rows - 1)
+    second = jnp.where(odd, tile_rows - 1, 0)
+    chunks = tile_cols // LANES
+    row_copies = []
+    for j in range(chunks):
+        for which, row in enumerate((first, second)):
+            row_copies.append(
+                pltpu.make_async_copy(
+                    ice.at[:, row, pl.ds(j * LANES, LANES)],
+                    edge_rows.at[which, j, pl.ds(0, planes), :],
+                    row_sem.at[which, j],
+                )
+            )
+    send_copies = [
+        pltpu.make_async_copy(edge_rows.at[which], out, send_sem.at[which])
+        for which, out in enumerate((rows_a, rows_b))
+    ]
+    for copy in row_copies:
+        copy.start()
+    col_copies = []
     for p in range(NCAT):
         own = pl.ds(p * NFSD, NFSD)
-        for side, (buf, start) in enumerate(((west_buf, 0), (east_buf, tile_cols - LANES))):
-            col_copies.append(
+        col_copies.append(
+            [
                 pltpu.make_async_copy(
-                    ice.at[own, :, pl.ds(start, LANES)], buf.at[own], col_sem.at[side, p]
+                    ice.at[own, pl.ds(row, SUB), pl.ds(start, LANES)],
+                    buf.at[own, pl.ds(e * SUB, SUB), :],
+                    col_sem.at[p, side, e],
                 )
-            )
+                for side, (buf, start) in enumerate(
+                    ((west_buf, 0), (east_buf, tile_cols - LANES))
+                )
+                for e, row in enumerate((0, tile_rows - SUB))
+            ]
+        )
     groups = wave_sem.shape[0]
     step = dests // groups
+    wave_copies = []
     for p in range(groups):
         own = pl.ds(p * step, step)
         wave_copies.append(
             pltpu.make_async_copy(wave.at[:, own, :], wave_buf.at[:, own, :], wave_sem.at[p])
         )
-    odd = lax.rem(me_l, 2) == 1
-    first = jnp.where(odd, 0, tile_rows - 1)
-    second = jnp.where(odd, tile_rows - 1, 0)
-    row_copies = []
-    for j in range(chunks):
-        for which, (row, out) in enumerate(((first, rows_a), (second, rows_b))):
-            row_copies.append(
-                pltpu.make_async_copy(
-                    ice.at[:, row, pl.ds(j * LANES, LANES)],
-                    out.at[j, pl.ds(0, planes), :],
-                    row_sem.at[which, j],
-                )
-            )
-    for copy in col_copies + wave_copies + row_copies:
+    route_copy = pltpu.make_async_copy(route_hbm, route, route_sem)
+    route_copy.start()
+    for copies in col_copies + [wave_copies]:
+        for copy in copies:
+            copy.start()
+
+    ends = gather_edges(west_buf, east_buf, col_copies, planes, (0, SUB))
+    for copy in row_copies:
+        copy.wait()
+    for copy in send_copies:
         copy.start()
-
-    lane = lax.broadcasted_iota(jnp.int32, (SUB, LANES), 1)
-    columns = [jnp.zeros((SUB, LANES), jnp.float32) for _ in range(2 * bands)]
-    for p in range(planes):
-        if p % NFSD == 0:
-            for copy in col_copies[2 * (p // NFSD) : 2 * (p // NFSD) + 2]:
-                copy.wait()
-        for i in range(bands):
-            band = slice(SUB * i, SUB * i + SUB)
-            ends = jnp.where(lane == 0, west_buf[p, band, :], east_buf[p, band, :])
-            ends = pltpu.roll(ends, p, 1) if p else ends
-            columns[i] = jnp.where(lane == p, ends, columns[i])
-            columns[bands + i] = jnp.where(lane == (p - 1) % LANES, ends, columns[bands + i])
-    east = [pltpu.roll(part, 1, 1) for part in columns[bands:]]
-    for side, (parts_of, out) in enumerate(((columns[:bands], to_west), (east, to_east))):
-        for i in range(bands // 2):
-            out[SUB * i : SUB * i + SUB, :] = jnp.where(
-                lane < 64, parts_of[i], pltpu.roll(parts_of[bands // 2 + i], 64, 1)
-            )
-        corners[2 * side : 2 * side + 1, :] = parts_of[0][0:1, :]
-        corners[2 * side + 1 : 2 * side + 2, :] = parts_of[bands - 1][SUB - 1 : SUB, :]
+    for side in range(2):
+        corners[2 * side : 2 * side + 1, :] = ends[side][0][0:1, :]
+        corners[2 * side + 1 : 2 * side + 2, :] = ends[side][1][SUB - 1 : SUB, :]
 
     for group in range(dests // SUB):
         band = slice(SUB * group, SUB * group + SUB)
@@ -110,6 +131,7 @@
                 total = total + wave_buf[f, band, chunk] * np.float32((f + 1.0) / freq_count)
             sums[j, band, :] = total
 
+    route_copy.wait()
     side_of = []
     for to_b in range(blk_count):
         last_col = (to_b == lax.rem(me_b + 1, blk_count)) | (
@@ -123,46 +145,119 @@
             message[to, :, LANES * j : LANES * j + LANES] = sums[j, m : m + 1, :]
         which = side_of[m // lat_count] + row_of[m % lat_count]
         message[m, :, cells : cells + LANES] = corners[pl.ds(which, 1), :]
-    for copy in row_copies:
+    for copy in send_copies:
         copy.wait()
 
 
-def pack(ice, wave, route, blk_count, lat_count):
+def pack_wave(ice, wave, route, blk_count, lat_count):
     planes, tile_rows, tile_cols = ice.shape
     freq_count, dests, cells = wave.shape
     chunks = tile_cols // LANES
     hbm = pl.BlockSpec(memory_space=pl.ANY)
-    vmem = pl.BlockSpec(memory_space=pltpu.VMEM)
-    rows = jax.ShapeDtypeStruct((chunks, 64, LANES), jnp.float32)
-    column = jax.ShapeDtypeStruct((tile_rows // 2, LANES), jnp.float32)
     return pl.pallas_call(
-        functools.partial(pack_kernel, blk_count, lat_count),
+        functools.partial(wave_kernel, blk_count, lat_count),
         out_shape=(
             jax.ShapeDtypeStruct((dests, 1, cells + LANES), jnp.float32),
-            rows, rows, column, column,
+            pltpu.HBM((chunks, 64, LANES), jnp.float32),
+            pltpu.HBM((chunks, 64, LANES), jnp.float32),
         ),
-        in_specs=[hbm, hbm, pl.BlockSpec(memory_space=pltpu.SMEM)],
-        out_specs=(vmem,) * 5,
+        in_specs=[hbm] * 3,
+        out_specs=(pl.BlockSpec(memory_space=pltpu.VMEM), hbm, hbm),
         scratch_shapes=[
+            pltpu.VMEM((2, chunks, 64, LANES), jnp.float32),
+            pltpu.SMEM(route.shape, jnp.int32),
             pltpu.VMEM((freq_count, dests, cells), jnp.float32),
+            pltpu.VMEM((planes, 2 * SUB, LANES), jnp.float32),
+            pltpu.VMEM((planes, 2 * SUB, LANES), jnp.float32),
+            pltpu.VMEM((cells // LANES, dests, LANES), jnp.float32),
+            pltpu.VMEM((SUB, LANES), jnp.float32),
+            pltpu.SemaphoreType.DMA,
+            pltpu.SemaphoreType.DMA((4,)),
+            pltpu.SemaphoreType.DMA((NCAT, 2, 2)),
+            pltpu.SemaphoreType.DMA((2, chunks)),
+            pltpu.SemaphoreType.DMA((2,)),
+        ],
+        compiler_params=pltpu.CompilerParams(vmem_limit_bytes=VMEM_LIMIT),
+        name="pack_wave",
+    )(*[pltpu.with_memory_space_constraint(array, pltpu.HBM) for array in (wave, ice, route)])
+
+
+def halo_kernel(ice, after, to_west, to_east, west_buf, east_buf, col_sem):
+    planes, tile_rows, tile_cols = ice.shape
+    bands = tile_rows // SUB
+    col_copies = []
+    for p in range(NCAT):
+        own = pl.ds(p * NFSD, NFSD)
+        col_copies.append(
+            [
+                pltpu.make_async_copy(
+                    ice.at[own, :, pl.ds(start, LANES)], buf.at[own], col_sem.at[p, side]
+                )
+                for side, (buf, start) in enumerate(
+                    ((west_buf, 0), (east_buf, tile_cols - LANES))
+                )
+            ]
+        )
+    for copies in col_copies:
+        for copy in copies:
+            copy.start()
+
+    lane = lax.broadcasted_iota(jnp.int32, (SUB, LANES), 1)
+    ends = gather_edges(
+        west_buf, east_buf, col_copies, planes, tuple(range(0, tile_rows, SUB))
+    )
+    for parts_of, out in zip(ends, (to_west, to_east)):
+        for i in range(bands // 2):
+            out[SUB * i : SUB * i + SUB, :] = jnp.where(
+                lane < 64, parts_of[i], pltpu.roll(parts_of[bands // 2 + i], 64, 1)
+            )
+
+
+def pack_halo(ice, after):
+    planes, tile_rows, tile_cols = ice.shape
+    hbm = pl.BlockSpec(memory_space=pl.ANY)
+    vmem = pl.BlockSpec(memory_space=pltpu.VMEM)
+    column = pltpu.VMEM((tile_rows // 2, LANES), jnp.float32)
+    return pl.pallas_call(
+        halo_kernel,
+        out_shape=(column, column),
+        in_specs=[hbm, hbm],
+        out_specs=(vmem,) * 2,
+        scratch_shapes=[
             pltpu.VMEM((planes, tile_rows, LANES), jnp.float32),
             pltpu.VMEM((planes, tile_rows, LANES), jnp.float32),
-            pltpu.VMEM((cells // LANES, dests, LANES), jnp.float32),
-            pltpu.VMEM((SUB, LANES), jnp.float32),
-            pltpu.SemaphoreType.DMA((4,)),
-            pltpu.SemaphoreType.DMA((2, NCAT)),
-            pltpu.SemaphoreType.DMA((2, chunks)),
+            pltpu.SemaphoreType.DMA((NCAT, 2)),
         ],
         compiler_params=pltpu.CompilerParams(vmem_limit_bytes=VMEM_LIMIT),
-        name="pack",
-    )(wave, ice, route)
+        name="pack_halo",
+    )(*[pltpu.with_memory_space_constraint(array, pltpu.HBM) for array in (ice, after)])
+
+
+def shifted(pieces, west, east):
+    lane = lax.broadcasted_iota(jnp.int32, (SUB, LANES), 1)
+    chunks = len(pieces)
+    to_right = [pltpu.roll(piece, 1, 1) for piece in pieces]
+    to_left = [pltpu.roll(piece, LANES - 1, 1) for piece in pieces]
+    from_west = [to_right[0] if west is None else jnp.where(lane == 0, west, to_right[0])] + [
+        jnp.where(lane == 0, to_right[j - 1], to_right[j]) for j in range(1, chunks)
+    ]
+    from_east = [
+        jnp.where(lane == LANES - 1, to_left[j + 1], to_left[j]) for j in range(chunks - 1)
+    ]
+    from_east.append(
+        to_left[-1] if east is None else jnp.where(lane == LANES - 1, east, to_left[-1])
+    )
+    return from_west, pieces, from_east
 
 
 def step_kernel(
     blk_count, lat_count, cells,
-    cover, ice, weights, weld, received, rows_a, rows_b, west_col, east_col, table, out,
+    ice, weights, cover_hbm, weld_hbm, received_hbm, rows_a_hbm, rows_b_hbm, west_hbm, east_hbm,
+    table_hbm, out,
+    cover, weld, received, rows_a, rows_b, west_col, east_col, table,
     ice_buf, out_buf, weight_buf, ext_even, ext_odd, scaled, weld_now, rate, ghosts, cols,
-    moved_even, moved_odd, stacked_even, stacked_odd, exchange_table, ice_sem, weight_sem, out_sem,
+    moved_even, moved_odd, stacked_even, stacked_odd, exchange_table,
+    small_sem, ice_sem, weight_sem, out_sem,
 ):
     tile_rows, tile_cols = weld.shape
     bands = tile_rows // SUB
@@ -179,6 +274,16 @@
     def category(n):
         return pl.ds(n * NFSD, NFSD)
 
+    small_copies = [
+        pltpu.make_async_copy(source, to, small_sem.at[c])
+        for c, (source, to) in enumerate(
+            (
+                (rows_a_hbm, rows_a), (rows_b_hbm, rows_b), (west_hbm, west_col),
+                (east_hbm, east_col), (received_hbm, received), (cover_hbm, cover),
+                (weld_hbm, weld), (table_hbm, table),
+            )
+        )
+    ]
     ice_copies = [
         pltpu.make_async_copy(ice.at[category(n)], ice_buf.at[category(n)], ice_sem.at[n])
         for n in range(NCAT)
@@ -186,25 +291,15 @@
     weight_copy = pltpu.make_async_copy(weights, weight_buf, weight_sem)
     out_copies = [
         pltpu.make_async_copy(out_buf.at[category(n)], out.at[category(n)], out_sem.at[n])
-        for n in range(NCAT)
+        for n in range(NCAT - 1)
     ]
+    for copy in small_copies:
+        copy.start()
     ice_copies[0].start()
     weight_copy.start()
-    for copy in ice_copies[1:]:
-        copy.start()
-
-    def shifted(pieces, west, east):
-        to_right = [pltpu.roll(piece, 1, 1) for piece in pieces]
-        to_left = [pltpu.roll(piece, LANES - 1, 1) for piece in pieces]
-        from_west = [
-            jnp.where(lane == 0, to_right[j - 1] if j else west, to_right[j])
-            for j in range(chunks)
-        ]
-        from_east = [
-            jnp.where(lane == LANES - 1, to_left[j + 1] if j + 1 < chunks else east, to_left[j])
-            for j in range(chunks)
-        ]
-        return from_west, pieces, from_east
+    ice_copies[1].start()
+    for copy in small_copies:
+        copy.wait()
 
     top = me_l == lat_count - 1
     bottom = me_l == 0
@@ -379,43 +474,69 @@
                         widen(n + 1, (t + s) * per_tile + u)
 
     exchange_table[...] = table[...].astype(jnp.bfloat16)
+    ice_copies[0].wait()
+    border(0)
+
+    def first_units(u, _):
+        widen(0, u)
+        return 0
+
+    lax.fori_loop(0, bands * NFSD, first_units, 0, unroll=2)
     weight_copy.wait()
     for w in range(9):
         scaled[w] = weight_buf[w].astype(jnp.float32) * np.float32(1.0 / 4096.0)
-    ice_copies[0].wait()
-    border(0)
-
-    def first_units(u, _):
-        widen(0, u)
-        return 0
-
-    lax.fori_loop(0, bands * NFSD, first_units, 0, unroll=2)
     stencil(0, 0, 0)
     for n in range(NCAT):
         if n + 1 < NCAT:
             ice_copies[n + 1].wait()
+            if n + 2 < NCAT:
+                ice_copies[n + 2].start()
             border(n + 1)
 
-        def both(h, _):
-            pair(n, h * 2, False)
-            return 0
-
-        lax.fori_loop(0, tiles // 2 - 1, both, 0)
-        pair(n, tiles - 2, True)
-        out_copies[n].start()
+            def both(h, _):
+                pair(n, h * 2, False)
+                return 0
+
+            lax.fori_loop(0, tiles // 2 - 1, both, 0)
+            pair(n, tiles - 2, True)
+            out_copies[n].start()
+        else:
+
+            def band_copy(i):
+                rows = pl.ds(pl.multiple_of(i * SUB, SUB), SUB)
+                return pltpu.make_async_copy(
+                    out_buf.at[category(n), rows, :], out.at[category(n), rows, :],
+                    out_sem.at[n + i],
+                )
+
+            def one_band(i, _):
+                for h in range(per_band // 2):
+                    pair(n, i * per_band + h * 2, False)
+                band_copy(i).start()
+                return 0
+
+            lax.fori_loop(0, bands - 1, one_band, 0)
+            for h in range(per_band // 2 - 1):
+                pair(n, tiles - per_band + h * 2, False)
+            pair(n, tiles - 2, True)
+            band_copy(bands - 1).start()
+            for i in range(bands):
+                band_copy(i).wait()
     for copy in out_copies:
         copy.wait()
 
 
 def advance(
-    cover, ice, weights, weld, received, rows_a, rows_b, west_col, east_col,
+    cover, ice, weld, received, rows_a, rows_b, west_col, east_col, weights,
     blk_count, lat_count, cells,
 ):
     planes, tile_rows, tile_cols = ice.shape
     chunks = tile_cols // LANES
+    bands = tile_rows // SUB
     table = jnp.asarray(weld_table().astype(np.float32))
-    vmem = pl.BlockSpec(memory_space=pltpu.VMEM)
     hbm = pl.BlockSpec(memory_space=pl.ANY)
+    small = [cover, weld, received, rows_a, rows_b, west_col, east_col, table]
+    held = [pltpu.with_memory_space_constraint(array, pltpu.HBM) for array in [ice, weights] + small]
     tile = pltpu.VMEM((tile_rows, tile_cols), jnp.float32)
     ext = pltpu.VMEM((3, NFSD * (chunks * EXT + 1), LANES), jnp.float32)
     moved = pltpu.VMEM((NFSD * SUB, 2 * LANES), jnp.float32)
@@ -423,9 +544,11 @@
     return pl.pallas_call(
         functools.partial(step_kernel, blk_count, lat_count, cells),
         out_shape=jax.ShapeDtypeStruct(ice.shape, jnp.float32),
-        in_specs=[pl.BlockSpec(memory_space=pltpu.SMEM), hbm, hbm] + [vmem] * 7,
+        in_specs=[hbm] * 10,
         out_specs=hbm,
         scratch_shapes=[
+            pltpu.SMEM(cover.shape, jnp.int32),
+            *[pltpu.VMEM(array.shape, jnp.float32) for array in small[1:]],
             pltpu.VMEM(ice.shape, jnp.float32),
             pltpu.VMEM(ice.shape, jnp.float32),
             pltpu.VMEM(weights.shape, jnp.int32),
@@ -436,13 +559,14 @@
             pltpu.VMEM((2, tile_rows, LANES), jnp.float32),
             moved, moved, stacked, stacked,
             pltpu.VMEM((NFSD * SUB, 2 * LANES), jnp.bfloat16),
+            pltpu.SemaphoreType.DMA((len(small),)),
             pltpu.SemaphoreType.DMA((NCAT,)),
             pltpu.SemaphoreType.DMA,
-            pltpu.SemaphoreType.DMA((NCAT,)),
+            pltpu.SemaphoreType.DMA((NCAT - 1 + bands,)),
         ],
         compiler_params=pltpu.CompilerParams(vmem_limit_bytes=VMEM_LIMIT),
         name="advance",
-    )(cover, ice, weights, weld, received, rows_a, rows_b, west_col, east_col, table)
+    )(*held)
 
 
 def on_device(ice_area, departure_weights, weld_rate, ice_cover, wave_ocean, ocean_route):
@@ -452,9 +576,8 @@
     assert lat_count % 2 == 0 and blk_count % 2 == 0 and blk_count > 2
     cells = wave_ocean.shape[3]
     ice = ice_area.reshape(cat_count * floe_count, tile_rows, tile_cols)
-    message, rows_a, rows_b, to_west, to_east = pack(
-        ice, wave_ocean[0], ocean_route, blk_count, lat_count
-    )
+    message, rows_a, rows_b = pack_wave(ice, wave_ocean[0], ocean_route, blk_count, lat_count)
+    to_west, to_east = pack_halo(ice, message)
     received = lax.all_to_all(message, AXES, split_axis=0, concat_axis=0, tiled=True)
 
     pairs_a, pairs_b = [], []
@@ -472,8 +595,8 @@
     west_col = lax.ppermute(to_east, "blk", ring)
     east_col = lax.ppermute(to_west, "blk", [(b, a) for a, b in ring])
     result = advance(
-        ice_cover.reshape(1, tile_rows), ice, departure_weights, weld_rate,
-        received, from_a, from_b, west_col, east_col, blk_count, lat_count, cells,
+        ice_cover.reshape(1, tile_rows), ice, weld_rate, received, from_a, from_b,
+        west_col, east_col, departure_weights, blk_count, lat_count, cells,
     )
     return result.reshape(ice_area.shape)
 

time: 45.9 us -> 42.8 us (0.932)
  waiting for transfers between devices: 4.87 us -> 2.94 us
  Pallas kernels: 26.7 us -> 25.4 us
    pallas_call x1, Pallas kernels: 21.7 us -> 19.3 us  [advance(): pl.pallas_call(functools.partial(step_kernel, blk_count, lat_count, cells...]
    ppermute x1, waiting for transfers between devices: 3.61 us -> 1.89 us  [on_device(): from_b = lax.ppermute(rows_b, AXES, pairs_b)]
    pallas_call x1 -> x2, Pallas kernels: 4.99 us -> 6.1 us  [the longest x1 4.18 us: pack_wave(): pl.pallas_call(functools.partial(wave_kernel, blk_count, lat_count), out_...]
  transfers between devices with their start and end apart: 5 -> 5, of which waited for: 2 -> 2; matrix products, arithmetic and copies ran while one was open for 0% -> 0% of each run, Pallas kernels for 0% -> 5%
where the time goes in v2:
time: 42.8 us; the launch traced here: 42.5 us
  Pallas kernels  25.4 us (59%)
  starting transfers between devices  13.3 us (31%)
  waiting for transfers between devices  2.94 us (7%)
  local copies, waits for them, and re-layouts  0.75 us (2%)
    pallas_call x1, Pallas kernels, advance(): pl.pallas_call(functools.partial(step_kernel, blk_count, lat_count, cells...  19.3 us
    all_to_all x1, starting transfers between devices, on_device(): lax.all_to_all(message, AXES, split_axis=0, concat_axis=0, tiled=True)  6.45 us
    pallas_call x1, Pallas kernels, pack_wave(): pl.pallas_call(functools.partial(wave_kernel, blk_count, lat_count), out_...  4.18 us
    ppermute x1, starting transfers between devices, on_device(): from_b = lax.ppermute(rows_b, AXES, pairs_b)  3.11 us
    ppermute x1, starting transfers between devices, on_device(): east_col = lax.ppermute(to_west, 'blk', [(b, a) for a, b in ring])  2.08 us
    pallas_call x1, Pallas kernels, pack_halo(): pl.pallas_call(halo_kernel, out_shape=(column, column), in_specs=[hbm, hb...  1.92 us
    ppermute x1, waiting for transfers between devices, on_device(): from_b = lax.ppermute(rows_b, AXES, pairs_b)  1.89 us
    ppermute x1, starting transfers between devices, on_device(): west_col = lax.ppermute(to_east, 'blk', ring)  1.24 us
  transfers between devices with their start and end apart: 5, of which 2 were waited for; matrix products, arithmetic and copies ran while one was open for 0% of the time, Pallas kernels for 5%

profile of v2, /device:TPU:3, one launch (start us, length us, event | category | flops | bytes accessed | tf_op | source)
XLA Modules:
  0.0 42.5 jit_solution(60558203018252212)
XLA Ops:
  0.0 4.2 %pack_wave.1 = (f32[32,1,1152]{2,1,0:T(1,128)}, f32[8,64,128]{2,1,0:T(8,128)}, f32[8,64,128]{2,1,0:T(8,128)}) custom-call(f32[25,32,1024]{2,1,0:T(8,128)} %bitcast.7, f32[60,32,1024]{2,1,0:T(8,128)} %bitcast.4, s32[1,32]{1,0:T(1,128)} %route_hbm.1), custom_call_target="tpu_custom_call" | custom-call | tf_op jit(solution)/shard_map/pack_wave/pallas_call | solution.py:157
  4.2 6.4 %all-to-all-start = ((f32[32,1,1152]{2,1,0:T(1,128)}), f32[32,1,1152]{2,1,0:T(1,128)S(1)}, u32[]{:S(2)}, u32[]{:S(2)}) async-start(f32[32,1,1152]{2,1,0:T(1,128)} %get-tuple-element.10.after), calls=%async_computation | async-start | bytes 294912 | tf_op jit(solution)/shard_map/all_to_all | solution.py:581
  10.6 0.4 %collective-permute-start = (f32[8,64,128]{2,1,0:T(8,128)}, f32[8,64,128]{2,1,0:T(8,128)S(1)}, u32[]{:S(2)}, u32[]{:S(2)}) collective-permute-start(f32[8,64,128]{2,1,0:T(8,128)} %get-tuple-element.11), channel_id=1, source_target_pairs={{0,1},{1,0},{2,3},{3,2},{4,5},{5,4},{6,7},{7,6},{8,9},{9,8},{10,11... | collective-permute-start | bytes 786440 | tf_op jit(solution)/shard_map/ppermute | solution.py:592
  11.1 3.1 %collective-permute-start.1 = (f32[8,64,128]{2,1,0:T(8,128)}, f32[8,64,128]{2,1,0:T(8,128)S(1)}, u32[]{:S(2)}, u32[]{:S(2)}) collective-permute-start(f32[8,64,128]{2,1,0:T(8,128)} %get-tuple-element.12), channel_id=1, source_target_pairs={{1,2},{2,1},{3,4},{4,3},{5,6},{6,5},{7,31},{9,10},{10,9},{11,12},{... | collective-permute-start | bytes 786440 | tf_op jit(solution)/shard_map/ppermute | solution.py:593
  14.2 1.9 %pack_halo.1 = (f32[16,128]{1,0:T(8,128)S(1)}, f32[16,128]{1,0:T(8,128)S(1)}) custom-call(f32[60,32,1024]{2,1,0:T(8,128)} %bitcast.5, f32[32,1,1152]{2,1,0:T(1,128)} %get-tuple-element.10.after), custom_call_target="tpu_custom_call" | custom-call | tf_op jit(solution)/shard_map/pack_halo/pallas_call | solution.py:221
  16.1 1.2 %collective-permute-start.2 = (f32[16,128]{1,0:T(8,128)S(1)}, f32[16,128]{1,0:T(8,128)S(1)}, u32[]{:S(2)}, u32[]{:S(2)}) collective-permute-start(f32[16,128]{1,0:T(8,128)S(1)} %get-tuple-element.13), channel_id=1, source_target_pairs={{0,8},{8,16},{16,24},{24,0},{1,9},{9,17},{17,25},{25,1},{2,10},{10... | collective-permute-start | bytes 24584 | tf_op jit(solution)/shard_map/ppermute | solution.py:595
  17.4 2.1 %collective-permute-start.3 = (f32[16,128]{1,0:T(8,128)S(1)}, f32[16,128]{1,0:T(8,128)S(1)}, u32[]{:S(2)}, u32[]{:S(2)}) collective-permute-start(f32[16,128]{1,0:T(8,128)S(1)} %get-tuple-element.14), channel_id=1, source_target_pairs={{8,0},{16,8},{24,16},{0,24},{9,1},{17,9},{25,17},{1,25},{10,2},{18... | collective-permute-start | bytes 24584 | tf_op jit(solution)/shard_map/ppermute | solution.py:596
  19.4 1.0 %collective-permute-done.2.west_hbm = f32[16,128]{1,0:T(8,128)S(1)} collective-permute-done((f32[16,128]{1,0:T(8,128)S(1)}, f32[16,128]{1,0:T(8,128)S(1)}, u32[]{:S(2)}, u32[]{:S(2)}) %collective-permute-start.2) | collective-permute-done | bytes 8224 | tf_op jit(solution)/shard_map/ppermute | solution.py:595
  20.5 0.0 copy-start.3
  20.5 0.0 collective-permute-done.3.east_hbm
  20.5 0.0 copy-start.4
  20.5 0.0 collective-permute-done.rows_a_hbm
  20.5 0.0 copy-start.1
  20.5 1.9 %collective-permute-done.1.rows_b_hbm = f32[8,64,128]{2,1,0:T(8,128)S(1)} collective-permute-done((f32[8,64,128]{2,1,0:T(8,128)}, f32[8,64,128]{2,1,0:T(8,128)S(1)}, u32[]{:S(2)}, u32[]{:S(2)}) %collective-permute-start.1) | collective-permute-done | bytes 262176 | tf_op jit(solution)/shard_map/ppermute | solution.py:593
  22.4 0.0 copy-start.2
  22.4 0.0 all-to-all-done.received_hbm
  22.4 0.0 copy-start
  22.4 0.0 copy-done.3
  22.4 0.0 copy-done.4
  22.4 0.0 copy-done.1
  22.4 0.7 %copy-done.2 = f32[8,64,128]{2,1,0:T(8,128)} copy-done((f32[8,64,128]{2,1,0:T(8,128)}, f32[8,64,128]{2,1,0:T(8,128)S(1)}, u32[]{:S(2)}) %copy-start.2) | copy-done | bytes 262168
  23.1 0.1 copy-done
  23.2 19.3 %advance.1 = f32[60,32,1024]{2,1,0:T(8,128)} custom-call(f32[60,32,1024]{2,1,0:T(8,128)} %bitcast.6, s32[9,32,1024]{2,1,0:T(8,128)} %weights.1, s32[1,32]{1,0:T(1,128)} %bitcast.8, f32[32,1024]{1,0:T(8,128)} %weld_hbm.1, f32[32,1,1152]{2,1,0:T(1,128)} %copy-done, f32[8,64,128]{2,1,0:T(8,128)} %copy-done.1, f32[8,64,128]{2,1,0:T(8,128)} %copy-done.2, ...), custom_call_target="tpu_custom_call" | custom-call | tf_op jit(solution)/shard_map/advance/pallas_call | solution.py:544
Async XLA Ops:
  4.2 18.2 %all-to-all-start = ((f32[32,1,1152]{2,1,0:T(1,128)}), f32[32,1,1152]{2,1,0:T(1,128)S(1)}, u32[]{:S(2)}, u32[]{:S(2)}) async-start(f32[32,1,1152]{2,1,0:T(1,128)} %get-tuple-element.10.after), calls=%async_computation | async-start | bytes 294912 | tf_op jit(solution)/shard_map/all_to_all | solution.py:581
  10.6 9.8 %collective-permute-start = (f32[8,64,128]{2,1,0:T(8,128)}, f32[8,64,128]{2,1,0:T(8,128)S(1)}, u32[]{:S(2)}, u32[]{:S(2)}) collective-permute-start(f32[8,64,128]{2,1,0:T(8,128)} %get-tuple-element.11), channel_id=1, source_target_pairs={{0,1},{1,0},{2,3},{3,2},{4,5},{5,4},{6,7},{7,6},{8,9},{9,8},{10,11... | collective-permute-start | bytes 786440 | tf_op jit(solution)/shard_map/ppermute | solution.py:592
  11.1 11.3 %collective-permute-start.1 = (f32[8,64,128]{2,1,0:T(8,128)}, f32[8,64,128]{2,1,0:T(8,128)S(1)}, u32[]{:S(2)}, u32[]{:S(2)}) collective-permute-start(f32[8,64,128]{2,1,0:T(8,128)} %get-tuple-element.12), channel_id=1, source_target_pairs={{1,2},{2,1},{3,4},{4,3},{5,6},{6,5},{7,31},{9,10},{10,9},{11,12},{... | collective-permute-start | bytes 786440 | tf_op jit(solution)/shard_map/ppermute | solution.py:593
  16.1 4.4 %collective-permute-start.2 = (f32[16,128]{1,0:T(8,128)S(1)}, f32[16,128]{1,0:T(8,128)S(1)}, u32[]{:S(2)}, u32[]{:S(2)}) collective-permute-start(f32[16,128]{1,0:T(8,128)S(1)} %get-tuple-element.13), channel_id=1, source_target_pairs={{0,8},{8,16},{16,24},{24,0},{1,9},{9,17},{17,25},{25,1},{2,10},{10... | collective-permute-start | bytes 24584 | tf_op jit(solution)/shard_map/ppermute | solution.py:595
  17.4 3.1 %collective-permute-start.3 = (f32[16,128]{1,0:T(8,128)S(1)}, f32[16,128]{1,0:T(8,128)S(1)}, u32[]{:S(2)}, u32[]{:S(2)}) collective-permute-start(f32[16,128]{1,0:T(8,128)S(1)} %get-tuple-element.14), channel_id=1, source_target_pairs={{8,0},{16,8},{24,16},{0,24},{9,1},{17,9},{25,17},{1,25},{10,2},{18... | collective-permute-start | bytes 24584 | tf_op jit(solution)/shard_map/ppermute | solution.py:596
  20.5 1.9 %copy-start.3 = (f32[16,128]{1,0:T(8,128)}, f32[16,128]{1,0:T(8,128)S(1)}, u32[]{:S(2)}) copy-start(f32[16,128]{1,0:T(8,128)S(1)} %collective-permute-done.2.west_hbm) | copy-start | bytes 24580
  20.5 1.9 %copy-start.4 = (f32[16,128]{1,0:T(8,128)}, f32[16,128]{1,0:T(8,128)S(1)}, u32[]{:S(2)}) copy-start(f32[16,128]{1,0:T(8,128)S(1)} %collective-permute-done.3.east_hbm) | copy-start | bytes 24580
  20.5 1.9 %copy-start.1 = (f32[8,64,128]{2,1,0:T(8,128)}, f32[8,64,128]{2,1,0:T(8,128)S(1)}, u32[]{:S(2)}) copy-start(f32[8,64,128]{2,1,0:T(8,128)S(1)} %collective-permute-done.rows_a_hbm) | copy-start | bytes 786436
  22.4 0.7 %copy-start.2 = (f32[8,64,128]{2,1,0:T(8,128)}, f32[8,64,128]{2,1,0:T(8,128)S(1)}, u32[]{:S(2)}) copy-start(f32[8,64,128]{2,1,0:T(8,128)S(1)} %collective-permute-done.1.rows_b_hbm) | copy-start | bytes 786436
  22.4 0.8 %copy-start = (f32[32,1,1152]{2,1,0:T(1,128)}, f32[32,1,1152]{2,1,0:T(1,128)S(1)}, u32[]{:S(2)}) copy-start(f32[32,1,1152]{2,1,0:T(1,128)S(1)} %all-to-all-done.received_hbm) | copy-start | bytes 442372

commit v3 on v2

--- a/solution.py
+++ b/solution.py
@@ -33,6 +33,20 @@
     assert not np.delete(low, kept, axis=1).any()
     joined = np.concatenate([high, high, low[:, kept]], axis=1)
     return np.kron(joined, np.eye(SUB)).astype(ml_dtypes.bfloat16)
+
+
+def turn_table():
+    right = np.roll(np.eye(LANES), 1, axis=1)
+    return np.tile(np.concatenate([right, right.T], axis=1), (2, 1)).astype(np.float32)
+
+
+def turned(whole, table):
+    high = whole.astype(jnp.bfloat16)
+    low = (whole - high.astype(jnp.float32)).astype(jnp.bfloat16)
+    both = jnp.dot(
+        jnp.concatenate([high, low], axis=1), table, preferred_element_type=jnp.float32
+    )
+    return both[:, :LANES], both[:, LANES:]
 
 
 def gather_edges(west_buf, east_buf, copies, planes, bands_of):
@@ -253,11 +267,11 @@
 def step_kernel(
     blk_count, lat_count, cells,
     ice, weights, cover_hbm, weld_hbm, received_hbm, rows_a_hbm, rows_b_hbm, west_hbm, east_hbm,
-    table_hbm, out,
-    cover, weld, received, rows_a, rows_b, west_col, east_col, table,
+    table_hbm, turning_hbm, out,
+    cover, weld, received, rows_a, rows_b, west_col, east_col, table, turning,
     ice_buf, out_buf, weight_buf, ext_even, ext_odd, scaled, weld_now, rate, ghosts, cols,
     moved_even, moved_odd, stacked_even, stacked_odd, exchange_table,
-    small_sem, ice_sem, weight_sem, out_sem,
+    lane_table, corner_lanes, small_sem, ice_sem, weight_sem, out_sem,
 ):
     tile_rows, tile_cols = weld.shape
     bands = tile_rows // SUB
@@ -280,7 +294,7 @@
             (
                 (rows_a_hbm, rows_a), (rows_b_hbm, rows_b), (west_hbm, west_col),
                 (east_hbm, east_col), (received_hbm, received), (cover_hbm, cover),
-                (weld_hbm, weld), (table_hbm, table),
+                (weld_hbm, weld), (table_hbm, table), (turning_hbm, turning),
             )
         )
     ]
@@ -333,8 +347,9 @@
         )
     ]
     backwards = LANES - 1 - lane
-    for q in range(SUB):
-        band = pl.ds(SUB * q, SUB)
+
+    def both_sides(q, _):
+        band = pl.ds(pl.multiple_of(SUB * q, SUB), SUB)
         below = [
             jnp.where(bottom, 0.0, jnp.where(odd, rows_a[j, band, :], rows_b[j, band, :]))
             for j in range(chunks)
@@ -344,13 +359,28 @@
             jnp.take_along_axis(above[chunks - 1 - j], backwards, axis=1) for j in range(chunks)
         ]
         above = [jnp.where(top, folded[j], above[j]) for j in range(chunks)]
-        for side, (pieces, corners) in enumerate(((below, below_corners), (above, above_corners))):
-            ends = [jnp.broadcast_to(corners[s][q], (SUB, LANES)) for s in range(2)]
-            if side == 0:
-                ends = [jnp.where(bottom, 0.0, end) for end in ends]
-            for dx, line in enumerate(shifted(pieces, *ends)):
-                for j in range(chunks):
-                    ghosts[side, dx, j, band, :] = line[j]
+        right, left = turned(jnp.concatenate(below + above, axis=0), lane_table[...])
+        for side, pieces in enumerate((below, above)):
+            at = [slice(SUB * c, SUB * c + SUB) for c in range(side * chunks, (side + 1) * chunks)]
+            to_right = [corner_lanes[2 * side, band, :]] + [right[c] for c in at]
+            to_left = [left[c] for c in at] + [corner_lanes[2 * side + 1, band, :]]
+            for j in range(chunks):
+                ghosts[side, 0, j, band, :] = jnp.where(lane == 0, to_right[j], to_right[j + 1])
+                ghosts[side, 1, j, band, :] = pieces[j]
+                ghosts[side, 2, j, band, :] = jnp.where(
+                    lane == LANES - 1, to_left[j + 1], to_left[j]
+                )
+        return 0
+
+    for side, corners in enumerate((below_corners, above_corners)):
+        for s in range(2):
+            for q in range(SUB):
+                end = jnp.broadcast_to(corners[s][q], (SUB, LANES))
+                if side == 0:
+                    end = jnp.where(bottom, 0.0, end)
+                corner_lanes[2 * side + s, SUB * q : SUB * q + SUB, :] = end
+    lane_table[...] = turning[...].astype(jnp.bfloat16)
+    lax.fori_loop(0, SUB, both_sides, 0, unroll=4)
 
     per_row = tile_cols // cells
     for r in range(tile_rows):
@@ -380,7 +410,33 @@
                             side, dx, j, pl.ds(n * NFSD + k0, SUB), :
                         ]
 
-    def widen(n, unit):
+    def widen(n, units):
+        ext = exts[n % 2]
+        pieces, places = [], []
+        for unit in units:
+            i = unit // NFSD
+            k = unit - i * NFSD
+            rows = pl.ds(pl.multiple_of(i * SUB, SUB), SUB)
+            places.append((i, k, rows))
+            pieces += [
+                ice_buf[n * NFSD + k, rows, LANES * j : LANES * j + LANES] for j in range(chunks)
+            ]
+        right, left = turned(jnp.concatenate(pieces, axis=0), lane_table[...])
+        for u, (i, k, rows) in enumerate(places):
+            p = n * NFSD + k
+            at = [slice(SUB * c, SUB * c + SUB) for c in range(u * chunks, (u + 1) * chunks)]
+            to_right = [pltpu.roll(cols[0, rows, :], LANES - p, 1)] + [right[c] for c in at]
+            to_left = [left[c] for c in at] + [pltpu.roll(cols[1, rows, :], LANES - 1 - p, 1)]
+            base = k * plane_pitch + SUB + i * SUB
+            for j in range(chunks):
+                own = pl.ds(base + j * EXT, SUB)
+                ext[0, own, :] = to_right[j + 1]
+                pltpu.store(ext.at[0, own, :], to_right[j], mask=lane == 0)
+                ext[1, own, :] = pieces[u * chunks + j]
+                ext[2, own, :] = to_left[j]
+                pltpu.store(ext.at[2, own, :], to_left[j + 1], mask=lane == LANES - 1)
+
+    def widen_by_rolls(n, unit):
         ext = exts[n % 2]
         i = unit // NFSD
         k = unit - i * NFSD
@@ -389,11 +445,18 @@
         pieces = [ice_buf[p, rows, LANES * j : LANES * j + LANES] for j in range(chunks)]
         west = pltpu.roll(cols[0, rows, :], LANES - p, 1)
         east = pltpu.roll(cols[1, rows, :], LANES - 1 - p, 1)
-        for dx, line in enumerate(shifted(pieces, west, east)):
-            for j in range(chunks):
-                ext[dx, pl.ds(k * plane_pitch + j * EXT + SUB + i * SUB, SUB), :] = line[j]
-
-    width = 2
+        to_right = [west] + [pltpu.roll(piece, 1, 1) for piece in pieces]
+        to_left = [pltpu.roll(piece, LANES - 1, 1) for piece in pieces] + [east]
+        base = k * plane_pitch + SUB + i * SUB
+        for j in range(chunks):
+            own = pl.ds(base + j * EXT, SUB)
+            ext[0, own, :] = to_right[j + 1]
+            pltpu.store(ext.at[0, own, :], to_right[j], mask=lane == 0)
+            ext[1, own, :] = pieces[j]
+            ext[2, own, :] = to_left[j]
+            pltpu.store(ext.at[2, own, :], to_left[j + 1], mask=lane == LANES - 1)
+
+    width = moved_even.shape[1] // LANES
     span = LANES * width
     per_band = chunks // width
     tiles = bands * per_band
@@ -430,31 +493,39 @@
         i, jj = place(t)
         rows = pl.ds(pl.multiple_of(i * SUB, SUB), SUB)
         columns = pl.ds(pl.multiple_of(jj * span, span), span)
-        speed = weld_now[rows, columns]
-        breaking = rate[rows, columns] * np.float32(1.0 / (1.0 + 0.5 * n))
-        own = [moved[SUB * k : SUB * k + SUB, :] for k in range(NFSD)]
-        squares = [area * (area * np.float32(weld_scale)) for area in own]
-        welded = []
-        for k in range(NFSD):
-            turn = own[k] * exchange[SUB * k : SUB * k + SUB, :]
-            if k:
-                turn = turn + squares[k - 1]
-            if k == NFSD - 1:
-                turn = turn + squares[k]
-            welded.append(own[k] + speed * turn)
-        carried = None
-        for k in range(NFSD - 1, -1, -1):
-            if k:
-                broken = breaking * welded[k]
-                change = broken * np.float32(-k)
-                if carried is not None:
-                    change = carried + change
-                carried = broken if carried is None else carried + broken
-            else:
+        share = np.float32(1.0 / (1.0 + 0.5 * n))
+        for s in range(width):
+            own_columns = slice(LANES * s, LANES * s + LANES)
+            columns = pl.ds(pl.multiple_of(jj * span + LANES * s, LANES), LANES)
+            speed = weld_now[rows, columns]
+            breaking = rate[rows, columns] * share
+            carried = None
+            area = moved[SUB * NFSD - SUB : SUB * NFSD, own_columns]
+            square = area * (area * np.float32(weld_scale))
+            for k in range(NFSD - 1, -1, -1):
+                turn = area * exchange[SUB * k : SUB * k + SUB, own_columns]
+                if k == NFSD - 1:
+                    turn = turn + square
+                if k:
+                    below = moved[SUB * k - SUB : SUB * k, own_columns]
+                    square = below * (below * np.float32(weld_scale))
+                    turn = turn + square
+                welded = area + speed * turn
                 change = carried
-            out_buf[n * NFSD + k, rows, columns] = welded[k] + change
+                if k:
+                    broken = breaking * welded
+                    change = broken * np.float32(-k)
+                    if carried is not None:
+                        change = carried + change
+                    carried = broken if carried is None else carried + broken
+                    area = below
+                out_buf[n * NFSD + k, rows, columns] = welded + change
 
     per_tile = bands * NFSD // tiles
+
+    def ahead(n, t):
+        for u in range(per_tile):
+            widen_by_rolls(n, t * per_tile + u)
 
     def pair(n, t, last):
         more = n + 1 < NCAT
@@ -462,26 +533,25 @@
             exchange = exchange_of(s)
             if last and s == 1:
                 if more:
-                    for u in range(per_tile):
-                        widen(n + 1, (t + s) * per_tile + u)
+                    ahead(n + 1, t + s)
                     stencil(n + 1, 0, 0)
                 finish(n, t + s, s, exchange)
             else:
                 stencil(n, t + s + 1, 1 - s)
                 finish(n, t + s, s, exchange)
                 if more:
-                    for u in range(per_tile):
-                        widen(n + 1, (t + s) * per_tile + u)
+                    ahead(n + 1, t + s)
 
     exchange_table[...] = table[...].astype(jnp.bfloat16)
     ice_copies[0].wait()
     border(0)
 
     def first_units(u, _):
-        widen(0, u)
+        for half in range(2):
+            widen(0, [u * NFSD + half * (NFSD // 2) + v for v in range(NFSD // 2)])
         return 0
 
-    lax.fori_loop(0, bands * NFSD, first_units, 0, unroll=2)
+    lax.fori_loop(0, bands, first_units, 0)
     weight_copy.wait()
     for w in range(9):
         scaled[w] = weight_buf[w].astype(jnp.float32) * np.float32(1.0 / 4096.0)
@@ -534,17 +604,18 @@
     chunks = tile_cols // LANES
     bands = tile_rows // SUB
     table = jnp.asarray(weld_table().astype(np.float32))
+    turning = jnp.asarray(turn_table())
     hbm = pl.BlockSpec(memory_space=pl.ANY)
-    small = [cover, weld, received, rows_a, rows_b, west_col, east_col, table]
+    small = [cover, weld, received, rows_a, rows_b, west_col, east_col, table, turning]
     held = [pltpu.with_memory_space_constraint(array, pltpu.HBM) for array in [ice, weights] + small]
     tile = pltpu.VMEM((tile_rows, tile_cols), jnp.float32)
     ext = pltpu.VMEM((3, NFSD * (chunks * EXT + 1), LANES), jnp.float32)
     moved = pltpu.VMEM((NFSD * SUB, 2 * LANES), jnp.float32)
-    stacked = pltpu.VMEM((2 * LANES, 2 * LANES), jnp.bfloat16)
+    stacked = pltpu.VMEM((table.shape[1], 2 * LANES), jnp.bfloat16)
     return pl.pallas_call(
         functools.partial(step_kernel, blk_count, lat_count, cells),
         out_shape=jax.ShapeDtypeStruct(ice.shape, jnp.float32),
-        in_specs=[hbm] * 10,
+        in_specs=[hbm] * len(held),
         out_specs=hbm,
         scratch_shapes=[
             pltpu.SMEM(cover.shape, jnp.int32),
@@ -559,6 +630,8 @@
             pltpu.VMEM((2, tile_rows, LANES), jnp.float32),
             moved, moved, stacked, stacked,
             pltpu.VMEM((NFSD * SUB, 2 * LANES), jnp.bfloat16),
+            pltpu.VMEM(turning.shape, jnp.bfloat16),
+            pltpu.VMEM((4, 64, LANES), jnp.float32),
             pltpu.SemaphoreType.DMA((len(small),)),
             pltpu.SemaphoreType.DMA((NCAT,)),
             pltpu.SemaphoreType.DMA,

time: 42.8 us -> 41.9 us (0.979)
  Pallas kernels: 25.4 us -> 24.5 us
    pallas_call x1, Pallas kernels: 19.3 us -> 18.4 us  [advance(): pl.pallas_call(functools.partial(step_kernel, blk_count, lat_count, cells...]
where the time goes in v3:
time: 41.9 us; the launch traced here: 41.6 us
  Pallas kernels  24.5 us (58%)
  starting transfers between devices  13.3 us (32%)
  waiting for transfers between devices  2.94 us (7%)
  local copies, waits for them, and re-layouts  0.75 us (2%)
    pallas_call x1, Pallas kernels, advance(): pl.pallas_call(functools.partial(step_kernel, blk_count, lat_count, cells...  18.4 us
    all_to_all x1, starting transfers between devices, on_device(): lax.all_to_all(message, AXES, split_axis=0, concat_axis=0, tiled=True)  6.45 us
    pallas_call x1, Pallas kernels, pack_wave(): pl.pallas_call(functools.partial(wave_kernel, blk_count, lat_count), out_...  4.18 us
    ppermute x1, starting transfers between devices, on_device(): from_b = lax.ppermute(rows_b, AXES, pairs_b)  3.11 us
    ppermute x1, starting transfers between devices, on_device(): east_col = lax.ppermute(to_west, 'blk', [(b, a) for a, b in ring])  2.08 us
    pallas_call x1, Pallas kernels, pack_halo(): pl.pallas_call(halo_kernel, out_shape=(column, column), in_specs=[hbm, hb...  1.92 us
    ppermute x1, waiting for transfers between devices, on_device(): from_b = lax.ppermute(rows_b, AXES, pairs_b)  1.89 us
    ppermute x1, starting transfers between devices, on_device(): west_col = lax.ppermute(to_east, 'blk', ring)  1.24 us
  transfers between devices with their start and end apart: 5, of which 2 were waited for; matrix products, arithmetic and copies ran while one was open for 0% of the time, Pallas kernels for 5%

profile of v3, /device:TPU:3, one launch (start us, length us, event | category | flops | bytes accessed | tf_op | source)
XLA Modules:
  0.0 41.6 jit_solution(9220537105169813324)
XLA Ops:
  0.0 4.2 %pack_wave.1 = (f32[32,1,1152]{2,1,0:T(1,128)}, f32[8,64,128]{2,1,0:T(8,128)}, f32[8,64,128]{2,1,0:T(8,128)}) custom-call(f32[25,32,1024]{2,1,0:T(8,128)} %bitcast.7, f32[60,32,1024]{2,1,0:T(8,128)} %bitcast.4, s32[1,32]{1,0:T(1,128)} %route_hbm.1), custom_call_target="tpu_custom_call" | custom-call | tf_op jit(solution)/shard_map/pack_wave/pallas_call | solution.py:171
  4.2 6.4 %all-to-all-start = ((f32[32,1,1152]{2,1,0:T(1,128)}), f32[32,1,1152]{2,1,0:T(1,128)S(1)}, u32[]{:S(2)}, u32[]{:S(2)}) async-start(f32[32,1,1152]{2,1,0:T(1,128)} %get-tuple-element.10.after), calls=%async_computation | async-start | bytes 294912 | tf_op jit(solution)/shard_map/all_to_all | solution.py:654
  10.6 0.4 %collective-permute-start = (f32[8,64,128]{2,1,0:T(8,128)}, f32[8,64,128]{2,1,0:T(8,128)S(1)}, u32[]{:S(2)}, u32[]{:S(2)}) collective-permute-start(f32[8,64,128]{2,1,0:T(8,128)} %get-tuple-element.11), channel_id=1, source_target_pairs={{0,1},{1,0},{2,3},{3,2},{4,5},{5,4},{6,7},{7,6},{8,9},{9,8},{10,11... | collective-permute-start | bytes 786440 | tf_op jit(solution)/shard_map/ppermute | solution.py:665
  11.1 3.1 %collective-permute-start.1 = (f32[8,64,128]{2,1,0:T(8,128)}, f32[8,64,128]{2,1,0:T(8,128)S(1)}, u32[]{:S(2)}, u32[]{:S(2)}) collective-permute-start(f32[8,64,128]{2,1,0:T(8,128)} %get-tuple-element.12), channel_id=1, source_target_pairs={{1,2},{2,1},{3,4},{4,3},{5,6},{6,5},{7,31},{9,10},{10,9},{11,12},{... | collective-permute-start | bytes 786440 | tf_op jit(solution)/shard_map/ppermute | solution.py:666
  14.2 1.9 %pack_halo.1 = (f32[16,128]{1,0:T(8,128)S(1)}, f32[16,128]{1,0:T(8,128)S(1)}) custom-call(f32[60,32,1024]{2,1,0:T(8,128)} %bitcast.5, f32[32,1,1152]{2,1,0:T(1,128)} %get-tuple-element.10.after), custom_call_target="tpu_custom_call" | custom-call | tf_op jit(solution)/shard_map/pack_halo/pallas_call | solution.py:235
  16.1 1.2 %collective-permute-start.2 = (f32[16,128]{1,0:T(8,128)S(1)}, f32[16,128]{1,0:T(8,128)S(1)}, u32[]{:S(2)}, u32[]{:S(2)}) collective-permute-start(f32[16,128]{1,0:T(8,128)S(1)} %get-tuple-element.13), channel_id=1, source_target_pairs={{0,8},{8,16},{16,24},{24,0},{1,9},{9,17},{17,25},{25,1},{2,10},{10... | collective-permute-start | bytes 24584 | tf_op jit(solution)/shard_map/ppermute | solution.py:668
  17.4 2.1 %collective-permute-start.3 = (f32[16,128]{1,0:T(8,128)S(1)}, f32[16,128]{1,0:T(8,128)S(1)}, u32[]{:S(2)}, u32[]{:S(2)}) collective-permute-start(f32[16,128]{1,0:T(8,128)S(1)} %get-tuple-element.14), channel_id=1, source_target_pairs={{8,0},{16,8},{24,16},{0,24},{9,1},{17,9},{25,17},{1,25},{10,2},{18... | collective-permute-start | bytes 24584 | tf_op jit(solution)/shard_map/ppermute | solution.py:669
  19.4 1.0 %collective-permute-done.2.west_hbm = f32[16,128]{1,0:T(8,128)S(1)} collective-permute-done((f32[16,128]{1,0:T(8,128)S(1)}, f32[16,128]{1,0:T(8,128)S(1)}, u32[]{:S(2)}, u32[]{:S(2)}) %collective-permute-start.2) | collective-permute-done | bytes 8224 | tf_op jit(solution)/shard_map/ppermute | solution.py:668
  20.5 0.0 copy-start.3
  20.5 0.0 collective-permute-done.3.east_hbm
  20.5 0.0 copy-start.4
  20.5 0.0 collective-permute-done.rows_a_hbm
  20.5 0.0 copy-start.1
  20.5 1.9 %collective-permute-done.1.rows_b_hbm = f32[8,64,128]{2,1,0:T(8,128)S(1)} collective-permute-done((f32[8,64,128]{2,1,0:T(8,128)}, f32[8,64,128]{2,1,0:T(8,128)S(1)}, u32[]{:S(2)}, u32[]{:S(2)}) %collective-permute-start.1) | collective-permute-done | bytes 262176 | tf_op jit(solution)/shard_map/ppermute | solution.py:666
  22.4 0.0 copy-start.2
  22.4 0.0 all-to-all-done.received_hbm
  22.4 0.0 copy-start
  22.4 0.0 copy-done.3
  22.4 0.0 copy-done.4
  22.4 0.0 copy-done.1
  22.4 0.7 %copy-done.2 = f32[8,64,128]{2,1,0:T(8,128)} copy-done((f32[8,64,128]{2,1,0:T(8,128)}, f32[8,64,128]{2,1,0:T(8,128)S(1)}, u32[]{:S(2)}) %copy-start.2) | copy-done | bytes 262168
  23.1 0.1 copy-done
  23.2 18.4 %advance.1 = f32[60,32,1024]{2,1,0:T(8,128)} custom-call(f32[60,32,1024]{2,1,0:T(8,128)} %bitcast.6, s32[9,32,1024]{2,1,0:T(8,128)} %weights.1, s32[1,32]{1,0:T(1,128)} %bitcast.8, f32[32,1024]{1,0:T(8,128)} %weld_hbm.1, f32[32,1,1152]{2,1,0:T(1,128)} %copy-done, f32[8,64,128]{2,1,0:T(8,128)} %copy-done.1, f32[8,64,128]{2,1,0:T(8,128)} %copy-done.2, ...), custom_call_target="tpu_custom_call" | custom-call | tf_op jit(solution)/shard_map/advance/pallas_call | solution.py:615
Async XLA Ops:
  4.2 18.2 %all-to-all-start = ((f32[32,1,1152]{2,1,0:T(1,128)}), f32[32,1,1152]{2,1,0:T(1,128)S(1)}, u32[]{:S(2)}, u32[]{:S(2)}) async-start(f32[32,1,1152]{2,1,0:T(1,128)} %get-tuple-element.10.after), calls=%async_computation | async-start | bytes 294912 | tf_op jit(solution)/shard_map/all_to_all | solution.py:654
  10.6 9.8 %collective-permute-start = (f32[8,64,128]{2,1,0:T(8,128)}, f32[8,64,128]{2,1,0:T(8,128)S(1)}, u32[]{:S(2)}, u32[]{:S(2)}) collective-permute-start(f32[8,64,128]{2,1,0:T(8,128)} %get-tuple-element.11), channel_id=1, source_target_pairs={{0,1},{1,0},{2,3},{3,2},{4,5},{5,4},{6,7},{7,6},{8,9},{9,8},{10,11... | collective-permute-start | bytes 786440 | tf_op jit(solution)/shard_map/ppermute | solution.py:665
  11.1 11.3 %collective-permute-start.1 = (f32[8,64,128]{2,1,0:T(8,128)}, f32[8,64,128]{2,1,0:T(8,128)S(1)}, u32[]{:S(2)}, u32[]{:S(2)}) collective-permute-start(f32[8,64,128]{2,1,0:T(8,128)} %get-tuple-element.12), channel_id=1, source_target_pairs={{1,2},{2,1},{3,4},{4,3},{5,6},{6,5},{7,31},{9,10},{10,9},{11,12},{... | collective-permute-start | bytes 786440 | tf_op jit(solution)/shard_map/ppermute | solution.py:666
  16.1 4.4 %collective-permute-start.2 = (f32[16,128]{1,0:T(8,128)S(1)}, f32[16,128]{1,0:T(8,128)S(1)}, u32[]{:S(2)}, u32[]{:S(2)}) collective-permute-start(f32[16,128]{1,0:T(8,128)S(1)} %get-tuple-element.13), channel_id=1, source_target_pairs={{0,8},{8,16},{16,24},{24,0},{1,9},{9,17},{17,25},{25,1},{2,10},{10... | collective-permute-start | bytes 24584 | tf_op jit(solution)/shard_map/ppermute | solution.py:668
  17.4 3.1 %collective-permute-start.3 = (f32[16,128]{1,0:T(8,128)S(1)}, f32[16,128]{1,0:T(8,128)S(1)}, u32[]{:S(2)}, u32[]{:S(2)}) collective-permute-start(f32[16,128]{1,0:T(8,128)S(1)} %get-tuple-element.14), channel_id=1, source_target_pairs={{8,0},{16,8},{24,16},{0,24},{9,1},{17,9},{25,17},{1,25},{10,2},{18... | collective-permute-start | bytes 24584 | tf_op jit(solution)/shard_map/ppermute | solution.py:669
  20.5 1.9 %copy-start.3 = (f32[16,128]{1,0:T(8,128)}, f32[16,128]{1,0:T(8,128)S(1)}, u32[]{:S(2)}) copy-start(f32[16,128]{1,0:T(8,128)S(1)} %collective-permute-done.2.west_hbm) | copy-start | bytes 24580
  20.5 1.9 %copy-start.4 = (f32[16,128]{1,0:T(8,128)}, f32[16,128]{1,0:T(8,128)S(1)}, u32[]{:S(2)}) copy-start(f32[16,128]{1,0:T(8,128)S(1)} %collective-permute-done.3.east_hbm) | copy-start | bytes 24580
  20.5 1.9 %copy-start.1 = (f32[8,64,128]{2,1,0:T(8,128)}, f32[8,64,128]{2,1,0:T(8,128)S(1)}, u32[]{:S(2)}) copy-start(f32[8,64,128]{2,1,0:T(8,128)S(1)} %collective-permute-done.rows_a_hbm) | copy-start | bytes 786436
  22.4 0.7 %copy-start.2 = (f32[8,64,128]{2,1,0:T(8,128)}, f32[8,64,128]{2,1,0:T(8,128)S(1)}, u32[]{:S(2)}) copy-start(f32[8,64,128]{2,1,0:T(8,128)S(1)} %collective-permute-done.1.rows_b_hbm) | copy-start | bytes 786436
  22.4 0.8 %copy-start = (f32[32,1,1152]{2,1,0:T(1,128)}, f32[32,1,1152]{2,1,0:T(1,128)S(1)}, u32[]{:S(2)}) copy-start(f32[32,1,1152]{2,1,0:T(1,128)S(1)} %all-to-all-done.received_hbm) | copy-start | bytes 442372

commit v4 on v3

--- a/solution.py
+++ b/solution.py
@@ -93,8 +93,6 @@
         pltpu.make_async_copy(edge_rows.at[which], out, send_sem.at[which])
         for which, out in enumerate((rows_a, rows_b))
     ]
-    for copy in row_copies:
-        copy.start()
     col_copies = []
     for p in range(NCAT):
         own = pl.ds(p * NFSD, NFSD)
@@ -121,15 +119,11 @@
         )
     route_copy = pltpu.make_async_copy(route_hbm, route, route_sem)
     route_copy.start()
-    for copies in col_copies + [wave_copies]:
+    for copies in col_copies + [wave_copies, row_copies]:
         for copy in copies:
             copy.start()
 
     ends = gather_edges(west_buf, east_buf, col_copies, planes, (0, SUB))
-    for copy in row_copies:
-        copy.wait()
-    for copy in send_copies:
-        copy.start()
     for side in range(2):
         corners[2 * side : 2 * side + 1, :] = ends[side][0][0:1, :]
         corners[2 * side + 1 : 2 * side + 2, :] = ends[side][1][SUB - 1 : SUB, :]
@@ -145,6 +139,10 @@
                 total = total + wave_buf[f, band, chunk] * np.float32((f + 1.0) / freq_count)
             sums[j, band, :] = total
 
+    for copy in row_copies:
+        copy.wait()
+    for copy in send_copies:
+        copy.start()
     route_copy.wait()
     side_of = []
     for to_b in range(blk_count):

time: 41.9 us -> 42.2 us (level)
  no operation moved by 1% of the time
where the time goes in v4:
time: 42.2 us; the launch traced here: 41.8 us
  Pallas kernels  24.8 us (59%)
  starting transfers between devices  13.3 us (32%)
  waiting for transfers between devices  2.94 us (7%)
  local copies, waits for them, and re-layouts  0.75 us (2%)
    pallas_call x1, Pallas kernels, advance(): pl.pallas_call(functools.partial(step_kernel, blk_count, lat_count, cells...  18.4 us
    all_to_all x1, starting transfers between devices, on_device(): lax.all_to_all(message, AXES, split_axis=0, concat_axis=0, tiled=True)  6.45 us
    pallas_call x1, Pallas kernels, pack_wave(): pl.pallas_call(functools.partial(wave_kernel, blk_count, lat_count), out_...  4.47 us
    ppermute x1, starting transfers between devices, on_device(): from_b = lax.ppermute(rows_b, AXES, pairs_b)  3.11 us
    ppermute x1, starting transfers between devices, on_device(): east_col = lax.ppermute(to_west, 'blk', [(b, a) for a, b in ring])  2.08 us
    pallas_call x1, Pallas kernels, pack_halo(): pl.pallas_call(halo_kernel, out_shape=(column, column), in_specs=[hbm, hb...  1.92 us
    ppermute x1, waiting for transfers between devices, on_device(): from_b = lax.ppermute(rows_b, AXES, pairs_b)  1.89 us
    ppermute x1, starting transfers between devices, on_device(): west_col = lax.ppermute(to_east, 'blk', ring)  1.24 us
  transfers between devices with their start and end apart: 5, of which 2 were waited for; matrix products, arithmetic and copies ran while one was open for 0% of the time, Pallas kernels for 5%

profile of v4, /device:TPU:3, one launch (start us, length us, event | category | flops | bytes accessed | tf_op | source)
XLA Modules:
  0.0 41.8 jit_solution(14048041414098810849)
XLA Ops:
  0.0 4.5 %pack_wave.1 = (f32[32,1,1152]{2,1,0:T(1,128)}, f32[8,64,128]{2,1,0:T(8,128)}, f32[8,64,128]{2,1,0:T(8,128)}) custom-call(f32[25,32,1024]{2,1,0:T(8,128)} %bitcast.7, f32[60,32,1024]{2,1,0:T(8,128)} %bitcast.4, s32[1,32]{1,0:T(1,128)} %route_hbm.1), custom_call_target="tpu_custom_call" | custom-call | tf_op jit(solution)/shard_map/pack_wave/pallas_call | solution.py:169
  4.5 6.4 %all-to-all-start = ((f32[32,1,1152]{2,1,0:T(1,128)}), f32[32,1,1152]{2,1,0:T(1,128)S(1)}, u32[]{:S(2)}, u32[]{:S(2)}) async-start(f32[32,1,1152]{2,1,0:T(1,128)} %get-tuple-element.10.after), calls=%async_computation | async-start | bytes 294912 | tf_op jit(solution)/shard_map/all_to_all | solution.py:652
  10.9 0.4 %collective-permute-start = (f32[8,64,128]{2,1,0:T(8,128)}, f32[8,64,128]{2,1,0:T(8,128)S(1)}, u32[]{:S(2)}, u32[]{:S(2)}) collective-permute-start(f32[8,64,128]{2,1,0:T(8,128)} %get-tuple-element.11), channel_id=1, source_target_pairs={{0,1},{1,0},{2,3},{3,2},{4,5},{5,4},{6,7},{7,6},{8,9},{9,8},{10,11... | collective-permute-start | bytes 786440 | tf_op jit(solution)/shard_map/ppermute | solution.py:663
  11.4 3.1 %collective-permute-start.1 = (f32[8,64,128]{2,1,0:T(8,128)}, f32[8,64,128]{2,1,0:T(8,128)S(1)}, u32[]{:S(2)}, u32[]{:S(2)}) collective-permute-start(f32[8,64,128]{2,1,0:T(8,128)} %get-tuple-element.12), channel_id=1, source_target_pairs={{1,2},{2,1},{3,4},{4,3},{5,6},{6,5},{7,31},{9,10},{10,9},{11,12},{... | collective-permute-start | bytes 786440 | tf_op jit(solution)/shard_map/ppermute | solution.py:664
  14.5 1.9 %pack_halo.1 = (f32[16,128]{1,0:T(8,128)S(1)}, f32[16,128]{1,0:T(8,128)S(1)}) custom-call(f32[60,32,1024]{2,1,0:T(8,128)} %bitcast.5, f32[32,1,1152]{2,1,0:T(1,128)} %get-tuple-element.10.after), custom_call_target="tpu_custom_call" | custom-call | tf_op jit(solution)/shard_map/pack_halo/pallas_call | solution.py:233
  16.4 1.2 %collective-permute-start.2 = (f32[16,128]{1,0:T(8,128)S(1)}, f32[16,128]{1,0:T(8,128)S(1)}, u32[]{:S(2)}, u32[]{:S(2)}) collective-permute-start(f32[16,128]{1,0:T(8,128)S(1)} %get-tuple-element.13), channel_id=1, source_target_pairs={{0,8},{8,16},{16,24},{24,0},{1,9},{9,17},{17,25},{25,1},{2,10},{10... | collective-permute-start | bytes 24584 | tf_op jit(solution)/shard_map/ppermute | solution.py:666
  17.7 2.1 %collective-permute-start.3 = (f32[16,128]{1,0:T(8,128)S(1)}, f32[16,128]{1,0:T(8,128)S(1)}, u32[]{:S(2)}, u32[]{:S(2)}) collective-permute-start(f32[16,128]{1,0:T(8,128)S(1)} %get-tuple-element.14), channel_id=1, source_target_pairs={{8,0},{16,8},{24,16},{0,24},{9,1},{17,9},{25,17},{1,25},{10,2},{18... | collective-permute-start | bytes 24584 | tf_op jit(solution)/shard_map/ppermute | solution.py:667
  19.7 1.0 %collective-permute-done.2.west_hbm = f32[16,128]{1,0:T(8,128)S(1)} collective-permute-done((f32[16,128]{1,0:T(8,128)S(1)}, f32[16,128]{1,0:T(8,128)S(1)}, u32[]{:S(2)}, u32[]{:S(2)}) %collective-permute-start.2) | collective-permute-done | bytes 8224 | tf_op jit(solution)/shard_map/ppermute | solution.py:666
  20.8 0.0 copy-start.3
  20.8 0.0 collective-permute-done.3.east_hbm
  20.8 0.0 copy-start.4
  20.8 0.0 collective-permute-done.rows_a_hbm
  20.8 0.0 copy-start.1
  20.8 1.9 %collective-permute-done.1.rows_b_hbm = f32[8,64,128]{2,1,0:T(8,128)S(1)} collective-permute-done((f32[8,64,128]{2,1,0:T(8,128)}, f32[8,64,128]{2,1,0:T(8,128)S(1)}, u32[]{:S(2)}, u32[]{:S(2)}) %collective-permute-start.1) | collective-permute-done | bytes 262176 | tf_op jit(solution)/shard_map/ppermute | solution.py:664
  22.7 0.0 copy-start.2
  22.7 0.0 all-to-all-done.received_hbm
  22.7 0.0 copy-start
  22.7 0.0 copy-done.3
  22.7 0.0 copy-done.4
  22.7 0.0 copy-done.1
  22.7 0.7 %copy-done.2 = f32[8,64,128]{2,1,0:T(8,128)} copy-done((f32[8,64,128]{2,1,0:T(8,128)}, f32[8,64,128]{2,1,0:T(8,128)S(1)}, u32[]{:S(2)}) %copy-start.2) | copy-done | bytes 262168
  23.4 0.1 copy-done
  23.5 18.4 %advance.1 = f32[60,32,1024]{2,1,0:T(8,128)} custom-call(f32[60,32,1024]{2,1,0:T(8,128)} %bitcast.6, s32[9,32,1024]{2,1,0:T(8,128)} %weights.1, s32[1,32]{1,0:T(1,128)} %bitcast.8, f32[32,1024]{1,0:T(8,128)} %weld_hbm.1, f32[32,1,1152]{2,1,0:T(1,128)} %copy-done, f32[8,64,128]{2,1,0:T(8,128)} %copy-done.1, f32[8,64,128]{2,1,0:T(8,128)} %copy-done.2, ...), custom_call_target="tpu_custom_call" | custom-call | tf_op jit(solution)/shard_map/advance/pallas_call | solution.py:613
Async XLA Ops:
  4.5 18.2 %all-to-all-start = ((f32[32,1,1152]{2,1,0:T(1,128)}), f32[32,1,1152]{2,1,0:T(1,128)S(1)}, u32[]{:S(2)}, u32[]{:S(2)}) async-start(f32[32,1,1152]{2,1,0:T(1,128)} %get-tuple-element.10.after), calls=%async_computation | async-start | bytes 294912 | tf_op jit(solution)/shard_map/all_to_all | solution.py:652
  10.9 9.8 %collective-permute-start = (f32[8,64,128]{2,1,0:T(8,128)}, f32[8,64,128]{2,1,0:T(8,128)S(1)}, u32[]{:S(2)}, u32[]{:S(2)}) collective-permute-start(f32[8,64,128]{2,1,0:T(8,128)} %get-tuple-element.11), channel_id=1, source_target_pairs={{0,1},{1,0},{2,3},{3,2},{4,5},{5,4},{6,7},{7,6},{8,9},{9,8},{10,11... | collective-permute-start | bytes 786440 | tf_op jit(solution)/shard_map/ppermute | solution.py:663
  11.4 11.3 %collective-permute-start.1 = (f32[8,64,128]{2,1,0:T(8,128)}, f32[8,64,128]{2,1,0:T(8,128)S(1)}, u32[]{:S(2)}, u32[]{:S(2)}) collective-permute-start(f32[8,64,128]{2,1,0:T(8,128)} %get-tuple-element.12), channel_id=1, source_target_pairs={{1,2},{2,1},{3,4},{4,3},{5,6},{6,5},{7,31},{9,10},{10,9},{11,12},{... | collective-permute-start | bytes 786440 | tf_op jit(solution)/shard_map/ppermute | solution.py:664
  16.4 4.4 %collective-permute-start.2 = (f32[16,128]{1,0:T(8,128)S(1)}, f32[16,128]{1,0:T(8,128)S(1)}, u32[]{:S(2)}, u32[]{:S(2)}) collective-permute-start(f32[16,128]{1,0:T(8,128)S(1)} %get-tuple-element.13), channel_id=1, source_target_pairs={{0,8},{8,16},{16,24},{24,0},{1,9},{9,17},{17,25},{25,1},{2,10},{10... | collective-permute-start | bytes 24584 | tf_op jit(solution)/shard_map/ppermute | solution.py:666
  17.7 3.1 %collective-permute-start.3 = (f32[16,128]{1,0:T(8,128)S(1)}, f32[16,128]{1,0:T(8,128)S(1)}, u32[]{:S(2)}, u32[]{:S(2)}) collective-permute-start(f32[16,128]{1,0:T(8,128)S(1)} %get-tuple-element.14), channel_id=1, source_target_pairs={{8,0},{16,8},{24,16},{0,24},{9,1},{17,9},{25,17},{1,25},{10,2},{18... | collective-permute-start | bytes 24584 | tf_op jit(solution)/shard_map/ppermute | solution.py:667
  20.8 1.9 %copy-start.3 = (f32[16,128]{1,0:T(8,128)}, f32[16,128]{1,0:T(8,128)S(1)}, u32[]{:S(2)}) copy-start(f32[16,128]{1,0:T(8,128)S(1)} %collective-permute-done.2.west_hbm) | copy-start | bytes 24580
  20.8 1.9 %copy-start.4 = (f32[16,128]{1,0:T(8,128)}, f32[16,128]{1,0:T(8,128)S(1)}, u32[]{:S(2)}) copy-start(f32[16,128]{1,0:T(8,128)S(1)} %collective-permute-done.3.east_hbm) | copy-start | bytes 24580
  20.8 1.9 %copy-start.1 = (f32[8,64,128]{2,1,0:T(8,128)}, f32[8,64,128]{2,1,0:T(8,128)S(1)}, u32[]{:S(2)}) copy-start(f32[8,64,128]{2,1,0:T(8,128)S(1)} %collective-permute-done.rows_a_hbm) | copy-start | bytes 786436
  22.7 0.7 %copy-start.2 = (f32[8,64,128]{2,1,0:T(8,128)}, f32[8,64,128]{2,1,0:T(8,128)S(1)}, u32[]{:S(2)}) copy-start(f32[8,64,128]{2,1,0:T(8,128)S(1)} %collective-permute-done.1.rows_b_hbm) | copy-start | bytes 786436
  22.7 0.8 %copy-start = (f32[32,1,1152]{2,1,0:T(1,128)}, f32[32,1,1152]{2,1,0:T(1,128)S(1)}, u32[]{:S(2)}) copy-start(f32[32,1,1152]{2,1,0:T(1,128)S(1)} %all-to-all-done.received_hbm) | copy-start | bytes 442372
